TPU v7x, 128 devices: a whole 4x4x4 slice. The times are simulated.
128 devices in a mesh: member: 8 (over x, core), mp: 16 (over y, z).
Axes of the slice: x: 4, y: 4, z: 4, core: 2. Of those that a mesh axis runs over, the one named last changes fastest.
Arguments:
- hidden: bfloat16 [8, 2048, 1024], P('member', 'mp'), may hold values from -6 to 6
- grid_emb: bfloat16 [8, 16384, 1024], P('member', 'mp'), may hold values from -6 to 6
- targets: float32 [100, 16384], P(None, 'mp'), may hold values from -6 to 6
- area_w: float32 [16384], P('mp'), may hold values from 1 to 10
- field_w: float32 [100], replicated, may hold values from 0.3 to 3
- edge_table: int32 [16384, 3], P('mp'), may hold values from 0 to 255, as said below
- halo_rows: int32 [64, 32], P('mp'), may hold values from 0 to 127, as said below
- w_query: bfloat16 [1024, 1024], replicated, may hold values from -0.1875 to 0.1875
- w_keyval: bfloat16 [2048, 1024], replicated, may hold values from -0.1875 to 0.1875
- w_attn_out: bfloat16 [1024, 1024], replicated, may hold values from -0.1875 to 0.1875
- w_fields: bfloat16 [100, 1024], replicated, may hold values from -0.1875 to 0.1875
Outputs:
- d_hidden: bfloat16 [8, 2048, 1024], P('member', 'mp')
- d_grid: bfloat16 [8, 16384, 1024], P('member', 'mp')
- grad_wq: float32 [1024, 1024], P(('member', 'mp'))
- grad_wkv: float32 [2048, 1024], P(('member', 'mp'))
- grad_wo: float32 [1024, 1024], P(('member', 'mp'))
- grad_wf: float32 [100, 1024], replicated
Inputs may be any that keep to these rules, and one draw needn't show every extreme that they name: `halo_rows`: the four rows of device d's block list the local hidden nodes (row numbers within d's 128) that d sends to the mp devices at offsets -2, -1, +1, +2 (cyclic), in that order. Each list holds distinct rows in its first L entries, L from 16 to 32, with L = 32 for some list, and zeros after them. `edge_table`: entries index a table of 256 rows on the point's device: below 128 the device's own hidden nodes; 128 + r * 32 + p is entry p of the list that the device at offset -2, -1, +1, +2 (r = 0 to 3) sends to this device, with p below that list's filled length.
All inputs are finite; a program needn't handle non-finite values.
Results may differ from a plain program's by a relative error of at most 0.035.
Values may be sent and summed in bfloat16 or wider, within the bound.
A program may use at most 192 MiB of HBM per device.

v0:
```python
import math

import jax
import jax.numpy as jnp
from jax import lax
from jax.sharding import PartitionSpec as P

HEADS = 16


ALPHA_FAIR = 0.95
KAPPA = 0.1
OFFSETS = (-2, -1, 1, 2)
CONTRACT_ROWS = (((0,), (0,)), ((), ()))
CONTRACT_LAST = (((1,), (1,)), ((), ()))
CONTRACT_INNER = (((1,), (0,)), ((), ()))


def shifted(x, axis, by):
    count = lax.axis_size(axis)
    return lax.ppermute(x, axis, [(i, (i + by) % count) for i in range(count)])


def soft_sign(value):
    return value / jnp.sqrt(value * value + KAPPA * KAPPA)


def product(left, right, numbers):
    return lax.dot_general(left, right, numbers, preferred_element_type=jnp.float32)


def fair_gradient(mine, ensemble, truth, scale, members, fair):
    spread = jnp.sum(soft_sign(mine[:, None] - ensemble[None]), axis=1)
    return scale * (soft_sign(mine - truth) / members - fair * spread)


def on_device(
    hidden,
    grid_emb,
    targets,
    area_w,
    field_w,
    edge_table,
    halo_rows,
    w_query,
    w_keyval,
    w_attn_out,
    w_fields,
):
    hidden_rows = hidden[0]
    grid_rows = grid_emb[0]
    local_nodes, width = hidden_rows.shape
    grid_count = grid_rows.shape[0]
    halo_width = halo_rows.shape[1]
    edges_each = edge_table.shape[1]
    head_dim = width // HEADS
    root = math.sqrt(head_dim)
    mp_count = lax.axis_size("mp")
    members = lax.axis_size("member")
    query = product(grid_rows, w_query, CONTRACT_LAST).astype(jnp.bfloat16)
    keyval = product(hidden_rows, w_keyval, CONTRACT_LAST).astype(jnp.bfloat16)
    outgoing = keyval[halo_rows]
    arrived = []
    for which in range(4):
        arrived.append(shifted(outgoing[3 - which], "mp", -OFFSETS[which]))
    incoming = jnp.stack(arrived)
    table = jnp.concatenate([keyval, incoming.reshape(4 * halo_width, 2 * width)], axis=0)
    picked = table[edge_table]
    keys = picked[:, :, :width].reshape(grid_count, edges_each, HEADS, head_dim)
    values = picked[:, :, width:].reshape(grid_count, edges_each, HEADS, head_dim)
    query_heads = query.reshape(grid_count, HEADS, head_dim)
    scores = (
        jnp.einsum("ghd,gkhd->gkh", query_heads, keys, preferred_element_type=jnp.float32) / root
    )
    raised = jnp.exp(scores)
    weights = raised / jnp.sum(raised, axis=1, keepdims=True)
    rounded = weights.astype(jnp.bfloat16)
    attended = jnp.einsum("gkh,gkhd->ghd", rounded, values, preferred_element_type=jnp.float32)
    attended = attended.reshape(grid_count, width).astype(jnp.bfloat16)
    mixed = (grid_rows.astype(jnp.float32) + product(attended, w_attn_out, CONTRACT_LAST)).astype(
        jnp.bfloat16
    )
    predicted = product(w_fields, mixed, CONTRACT_LAST)
    fair = (1.0 - (1.0 - ALPHA_FAIR) / members) / (members * (members - 1))
    ensemble = lax.all_gather(predicted[None], "member", axis=0, tiled=True)
    scale = field_w[:, None] * area_w[None, :]
    d_pred = fair_gradient(predicted[None], ensemble, targets, scale, members, fair)[0].astype(
        jnp.bfloat16
    )
    d_mixed = product(d_pred, w_fields, CONTRACT_ROWS).astype(jnp.bfloat16)
    field_terms = product(d_pred, mixed, CONTRACT_INNER)
    d_attended = product(d_mixed, w_attn_out, CONTRACT_INNER).reshape(grid_count, HEADS, head_dim)
    d_values = rounded.astype(jnp.float32)[..., None] * d_attended[:, None]
    d_weights = jnp.einsum("ghd,gkhd->gkh", d_attended, values, preferred_element_type=jnp.float32)
    d_scores = weights * (d_weights - jnp.sum(weights * d_weights, axis=1, keepdims=True))
    d_query = jnp.einsum("gkh,gkhd->ghd", d_scores, keys, preferred_element_type=jnp.float32) / root
    d_query = d_query.reshape(grid_count, width).astype(jnp.bfloat16)
    d_keys = d_scores[..., None] * query_heads.astype(jnp.float32)[:, None] / root
    table_rows = local_nodes + 4 * halo_width
    flat_edges = edge_table.reshape(-1)
    key_grads = jax.ops.segment_sum(
        d_keys.reshape(grid_count * edges_each, width), flat_edges, num_segments=table_rows
    )
    value_grads = jax.ops.segment_sum(
        d_values.reshape(grid_count * edges_each, width), flat_edges, num_segments=table_rows
    )
    table_grads = jnp.concatenate([key_grads, value_grads], axis=1)
    own_grads = table_grads[:local_nodes]
    returned = table_grads[local_nodes:].reshape(4, halo_width, 2 * width)
    coming = []
    for which in range(4):
        coming.append(shifted(returned[3 - which], "mp", -OFFSETS[which]))
    homecoming = jnp.stack(coming)
    node_grads = own_grads + jax.ops.segment_sum(
        homecoming.reshape(4 * halo_width, 2 * width),
        halo_rows.reshape(-1),
        num_segments=local_nodes,
    )
    node_grads = node_grads.astype(jnp.bfloat16)
    d_hidden = product(node_grads, w_keyval, CONTRACT_INNER).astype(jnp.bfloat16)
    d_grid = (d_mixed.astype(jnp.float32) + product(d_query, w_query, CONTRACT_INNER)).astype(
        jnp.bfloat16
    )
    norm = 1.0 / math.sqrt(members * mp_count * grid_count)
    query_terms = product(d_query, grid_rows, CONTRACT_ROWS)
    keyval_terms = product(node_grads, hidden_rows, CONTRACT_ROWS)
    out_terms = product(d_mixed, attended, CONTRACT_ROWS)
    grad_q, grad_kv, grad_o = (
        lax.psum_scatter(query_terms, ("member", "mp"), scatter_dimension=0, tiled=True),
        lax.psum_scatter(keyval_terms, ("member", "mp"), scatter_dimension=0, tiled=True),
        lax.psum_scatter(out_terms, ("member", "mp"), scatter_dimension=0, tiled=True),
    )
    grad_f = lax.psum(field_terms, ("member", "mp"))
    return (
        d_hidden[None],
        d_grid[None],
        grad_q * norm,
        grad_kv * norm,
        grad_o * norm,
        grad_f * norm,
    )


def solution(mesh):
    in_specs = (
        P("member", "mp", None),
        P("member", "mp", None),
        P(None, "mp"),
        P("mp"),
        P(),
        P("mp", None),
        P("mp", None),
        P(),
        P(),
        P(),
        P(),
    )
    out_specs = (
        P("member", "mp", None),
        P("member", "mp", None),
        P(("member", "mp"), None),
        P(("member", "mp"), None),
        P(("member", "mp"), None),
        P(),
    )
    return jax.shard_map(
        on_device, mesh=mesh, in_specs=in_specs, out_specs=out_specs, check_vma=False
    )
```

profile of v0, /device:TPU:1, one launch (start us, length us, event | category | flops | bytes accessed | tf_op | source)
XLA Modules:
  0.0 2241.5 jit_solution(7511117569400437091)
XLA Ops:
  8.1 3.8 convolution_convert_fusion
  13.6 4.4 collective-permute-start
  18.1 2.6 collective-permute-start.2
  20.7 2.4 collective-permute-start.3
  26.2 6.7 bitcast_convert_fusion.1
  35.1 16.4 gather_fusion.1
  51.6 32.4 %reshape.102 = bf16[1024,3,2048]{2,1,0:T(4,128)(2,1)} reshape(bf16[3072,2048]{1,0:T(8,128)(2,1)} %gather_fusion.1) | data formatting | bytes 25165824 | tf_op jit(solution)/shard_map/gather | solution.py:68
  83.9 15.7 fusion.28
  99.6 13.1 copy.60
  112.7 13.1 copy.59
  125.8 6.1 multiply_reduce_fusion.3
  131.9 1.7 copy.69
  133.6 6.2 convert_convert_fusion
  139.8 1.8 copy.64
  141.6 4.8 multiply_reduce_fusion.2
  146.4 2.4 add_convert_fusion.1
  152.0 29.4 %all-gather.4.cloned.1.call-done = f32[8,100,1024]{2,1,0:T(8,128)} async-done(((f32[1,100,1024]{2,1,0:T(8,128)}), f32[8,100,1024]{2,1,0:T(8,128)}) %all-gather.4.cloned.1.call-update) | async-done | bytes 3276816 | tf_op jit(solution)/shard_map/all_gather | solution.py:85
  181.4 2.9 multiply_reduce_fusion.4
  185.7 2.1 convolution_convert_fusion.1
  187.9 6.7 fusion.33
  194.6 4.1 fusion.32
  198.7 1.9 copy-done.3
  200.6 4.9 multiply_reduce_fusion.1
  205.6 1.7 copy.51
  207.3 5.0 fusion.2
  212.9 5.3 multiply_reduce_fusion
  220.2 4.3 fusion.4
  225.4 8.1 copy.29
  233.7 8.1 copy.30
  241.8 11.7 broadcast_multiply_fusion
  253.5 21.4 reshape.121
  274.9 11.2 multiply_multiply_fusion
  286.2 21.4 reshape.113
  307.5 27.9 %scatter_custom_fusion.1 = f32[256,1024]{1,0:T(8,128)S(1)} fusion(s32[3072]{0:T(1024)S(1)} %reshape.111, f32[3072,1024]{1,0:T(8,128)} %reshape.121, f32[]{:T(128)} %constant.8.clone.1), kind=kCustom, calls=%fused_computation.37 | custom fusion | flops 3145728 | bytes 1049088 | tf_op jit(solution)/shard_map/scatter-add | solution.py:104
  335.4 28.6 %scatter_custom_fusion = f32[256,1024]{1,0:T(8,128)} fusion(s32[3072]{0:T(1024)S(1)} %reshape.111, f32[3072,1024]{1,0:T(8,128)} %reshape.113, f32[]{:T(128)} %constant.8.clone.1), kind=kCustom, calls=%fused_computation.39 | custom fusion | flops 3145728 | bytes 1049088 | tf_op jit(solution)/shard_map/scatter-add | solution.py:101
  366.5 2.9 collective-permute-start.4
  369.4 2.2 collective-permute-start.7
  371.6 2.7 collective-permute-start.6
  374.7 7.2 collective-permute-done.4
  381.9 8.2 collective-permute-done.7
  393.0 2.6 scatter_fusion
  395.6 4.5 fusion.17
  400.1 6.7 fusion
  406.8 1.8 broadcast_multiply_fusion.1
  408.6 3.6 fusion.12
  412.2 533.7 %reduce-scatter.8.cloned.1.call-done = f32[8,1024]{1,0:T(8,128)} async-done(((f32[1024,1024]{1,0:T(8,128)}), f32[8,1024]{1,0:T(8,128)}) %reduce-scatter.8.cloned.1.call-update) | async-done | bytes 32784 | tf_op jit(solution)/shard_map/reduce_scatter | solution.py:131
  947.3 638.0 %reduce-scatter.4.cloned.1.call-done = f32[8,1024]{1,0:T(8,128)} async-done(((f32[1024,1024]{1,0:T(8,128)}), f32[8,1024]{1,0:T(8,128)}) %reduce-scatter.4.cloned.1.call-update) | async-done | bytes 32784 | tf_op jit(solution)/shard_map/reduce_scatter | solution.py:129
  1586.7 646.4 %reduce-scatter.6.cloned.1.call-done = f32[16,1024]{1,0:T(8,128)} async-done(((f32[2048,1024]{1,0:T(8,128)}), f32[16,1024]{1,0:T(8,128)}) %reduce-scatter.6.cloned.1.call-update) | async-done | bytes 65552 | tf_op jit(solution)/shard_map/reduce_scatter | solution.py:130
  (84 shorter events, 26.4 us)
Async XLA Ops:
  7.2 139.2 %copy-start = (bf16[1024,1024]{1,0:T(8,128)(2,1)S(1)}, bf16[1024,1024]{1,0:T(8,128)(2,1)}, u32[]{:S(2)}) copy-start(bf16[1024,1024]{1,0:T(8,128)(2,1)} %param.20) | copy-start | bytes 6291460
  7.2 174.2 %all-gather.4.cloned.1.call-start = ((), (), s32[]{:S(2)}) async-start(), calls=%async_computation.7 | async-start | bytes 3833856 | tf_op jit(solution)/shard_map/all_gather | solution.py:85
  11.9 14.3 copy-start.2
  13.6 19.2 collective-permute-start
  18.1 14.8 collective-permute-start.2
  20.7 12.2 collective-permute-start.1
  20.7 12.2 collective-permute-start.3
  26.2 6.7 copy-start.13
  141.6 4.8 copy-start.17
  146.4 2.4 copy-start.8
  146.4 3.7 copy-start.10
  148.8 1.3 copy-start.4
  150.2 34.1 %copy-start.11 = (f32[100,1024]{1,0:T(8,128)S(1)}, f32[100,1024]{1,0:T(8,128)}, u32[]{:S(2)}) copy-start(f32[100,1024]{1,0:T(8,128)} %param.13) | copy-start | bytes 1228804
  150.2 34.1 %copy-start.15 = (f32[1024]{0:T(1024)S(1)}, f32[1024]{0:T(1024)}, u32[]{:S(2)}) copy-start(f32[1024]{0:T(1024)} %param.14) | copy-start | bytes 12292
  150.2 34.1 %copy-start.16 = (f32[100]{0:T(128)S(1)}, f32[100]{0:T(128)}, u32[]{:S(2)}) copy-start(f32[100]{0:T(128)} %param.15) | copy-start | bytes 1204
  151.7 32.6 %copy-start.6 = (f32[1024,100]{0,1:T(8,128)S(1)}, f32[1024,100]{0,1:T(8,128)}, u32[]{:S(2)}) copy-start(f32[1024,100]{0,1:T(8,128)} %fusion.31) | copy-start | bytes 1228804
  151.7 255.1 %all-reduce.2.cloned.1.call-start = ((), (), s32[]{:S(2)}) async-start(), calls=%async_computation.6 | async-start | bytes 851968 | tf_op jit(solution)/shard_map/psum | solution.py:133
  181.4 3.1 copy-start.5
  187.8 758.1 %reduce-scatter.8.cloned.1.call-start = ((), (), s32[]{:S(2)}) async-start(), calls=%async_computation.5 | async-start | bytes 4227072 | tf_op jit(solution)/shard_map/reduce_scatter | solution.py:131
  194.6 1390.8 %reduce-scatter.4.cloned.1.call-start = ((), (), s32[]{:S(2)}) async-start(), calls=%async_computation.3 | async-start | bytes 4227072 | tf_op jit(solution)/shard_map/reduce_scatter | solution.py:129
  198.7 1.9 copy-start.3
  218.2 2.0 copy-start.18
  218.8 1.3 copy-start.7
  224.5 0.7 copy-start.12
  224.5 2008.6 %reduce-scatter.6.cloned.1.call-start = ((), (), s32[]{:S(2)}) async-start(), calls=%async_computation.4 | async-start | bytes 8454144 | tf_op jit(solution)/shard_map/reduce_scatter | solution.py:130
  364.1 10.5 copy-start.14
  366.5 15.4 collective-permute-start.4
  369.4 20.8 collective-permute-start.7
  371.6 20.2 collective-permute-start.6
  374.3 17.5 collective-permute-start.5
  393.0 2.6 copy-start.9
  400.1 1834.5 %copy-start.1 = (bf16[1024,1024]{1,0:T(8,128)(2,1)S(1)}, bf16[1024,1024]{1,0:T(8,128)(2,1)}, u32[]{:S(2)}) copy-start(bf16[1024,1024]{1,0:T(8,128)(2,1)} %param.20) | copy-start | bytes 6291460
Sparse Core Ops, SparseCore 0:
  151.9 29.4 all-gather.3
  187.9 142.3 all-reduce.1
  332.8 613.0 reduce-scatter.7
  948.2 637.0 reduce-scatter.3
  1587.6 645.3 reduce-scatter.5
where the time goes:
time: 2280 us; the launch traced here: 2240 us
  waiting for transfers between devices  1860 us (82%)
  local copies, waits for them, and re-layouts  167 us (7%)
  other arithmetic  130 us (6%)
  matrix products  47.5 us (2%)
    reduce_scatter x1, waiting for transfers between devices, on_device(): lax.psum_scatter(keyval_terms, ('member', 'mp'), scatter_dimension=0, til...  646 us
    reduce_scatter x1, waiting for transfers between devices, on_device(): lax.psum_scatter(query_terms, ('member', 'mp'), scatter_dimension=0, tile...  638 us
    reduce_scatter x1, waiting for transfers between devices, on_device(): lax.psum_scatter(out_terms, ('member', 'mp'), scatter_dimension=0, tiled=...  534 us
    gather x2, local copies, waits for them, and re-layouts, on_device(): picked = table[edge_table]  48.8 us
    dot_general x12, matrix products, product(): lax.dot_general(left, right, numbers, preferred_element_type=jnp.float32)  47.5 us
  transfers between devices with their start and end apart: 13, of which 7 were waited for; matrix products, arithmetic and copies ran while one was open for 9% of the time, Pallas kernels for 0%

commit v1 on v0

v1 whole, which is shorter than its diff:
```python
import functools
import math

import jax
import jax.numpy as jnp
from jax import lax
from jax.experimental import pallas as pl
from jax.experimental.pallas import tpu as pltpu
from jax.sharding import PartitionSpec as P

HEADS = 16
HEAD_DIM = 64
ALPHA_FAIR = 0.95
KAPPA = 0.1
OFFSETS = (-2, -1, 1, 2)
MEMBERS = 8
FIELD_ROWS = 112
LANES = 256
MESH = pl.DeviceIdType.MESH
BF16 = jnp.bfloat16
F32 = jnp.float32
NT = (((1,), (1,)), ((), ()))
NN = (((1,), (0,)), ((), ()))


def dot(left, right, numbers=NN):
    return lax.dot_general(left, right, numbers, preferred_element_type=F32)


def soft_sign(value):
    return value * lax.rsqrt(value * value + KAPPA * KAPPA)


def blocks(count, body):
    def step(at, carry):
        body(at)
        return carry

    lax.fori_loop(0, count, step, 0)


def kernel(
    hid_hbm, grid_hbm, tgt_ref, area_ref, field_ref, edge_ref, halo_ref,
    wq_hbm, wkv_hbm, wo_hbm, wf_ref,
    dhid_ref, dgrid_hbm, gq_ref, gkv_ref, go_ref, gf_ref,
    grid_v, wq_v, wkv_v, wo_v, wot_v, tgrid, qt, att, mix, th, tkv, oht, kvg, wts,
    wfp, wft, tpad, preds, predr, dps, dpr, dpf,
    datt, dkv_last, outgo, drecv,
    fs, fr1, fr2, fr3, fr4,
    send_buf, recv_buf,
    w_own, w_r1, w_s1, w_r2, w_fin,
    h_own, h_r1, h_s1, h_r2, h_fin,
    rx,
    load_sem, halo_s, halo_r, ps_s, ps_r, dp_s, dp_r, back_s, back_r,
    f1_s, f1_r, f2_s, f2_r, f3_s, f3_r, f4_s, f4_r,
    core_s, core_r, one_s, one_r, two_s, two_r, x_s, x_r, out_sem,
):
    me = lax.axis_index("member")
    mp = lax.axis_index("mp")
    x, c = lax.div(me, 2), lax.rem(me, 2)
    y, z = lax.div(mp, 4), lax.rem(mp, 4)
    other = 1 - c
    sibling = (2 * x + other, mp)
    norm = 1.0 / math.sqrt(MEMBERS * 16384.0)

    def halo_peer(by):
        return (me, lax.rem(mp + by + 16, 16))

    def member_peer(by):
        return lax.rem(me + by, 8)

    def y_peer(by):
        return (me, 4 * lax.rem(y + by, 4) + z)

    def z_peer(by):
        return (me, 4 * y + lax.rem(z + by, 4))

    def remote(src, dst, send, recv, device):
        return pltpu.make_async_remote_copy(
            src_ref=src, dst_ref=dst, send_sem=send, recv_sem=recv,
            device_id=device, device_id_type=MESH,
        )

    loads = [
        pltpu.make_async_copy(src, dst, load_sem.at[n])
        for n, (src, dst) in enumerate((
            (hid_hbm, th.at[pl.ds(0, 128)]), (grid_hbm, grid_v), (wq_hbm, wq_v),
            (wkv_hbm, wkv_v), (wo_hbm, wo_v),
        ))
    ]
    for load in loads:
        load.start()
    barrier = pltpu.get_barrier_semaphore()
    partners = (
        [halo_peer(by) for by in OFFSETS]
        + [(member_peer(by), mp) for by in range(1, 8)]
        + [y_peer(by) for by in range(1, 4)]
        + [z_peer(by) for by in range(1, 4)]
    )
    for partner in partners:
        pl.semaphore_signal(barrier, inc=1, device_id=partner, device_id_type=MESH)

    halo_hot = (
        halo_ref[...] == lax.broadcasted_iota(jnp.int32, (128, 128), 1)
    ).astype(BF16)
    loads[0].wait()
    outgo[...] = dot(halo_hot, th[pl.ds(0, 128), :]).astype(BF16)
    pl.semaphore_wait(barrier, len(partners))
    halos = []
    for l, by in enumerate(OFFSETS):
        copy = remote(
            outgo.at[pl.ds(32 * l, 32)], th.at[pl.ds(128 + 32 * (3 - l), 32)],
            halo_s.at[l], halo_r.at[3 - l], halo_peer(by),
        )
        copy.start()
        halos.append(copy)

    for e in range(3):
        def hot(at, e=e):
            rows = pl.ds(pl.multiple_of(at * 256, 256), 256)
            oht[e, rows, :] = (
                edge_ref[rows, e:e + 1] == lax.broadcasted_iota(jnp.int32, (256, 256), 1)
            ).astype(BF16)
        blocks(4, hot)
    wfp[...] = jnp.zeros_like(wfp)
    wfp[pl.ds(0, 100), :] = wf_ref[...]
    wft[...] = wfp[...].T
    tpad[...] = jnp.zeros_like(tpad)
    tpad[pl.ds(0, 100), :] = tgt_ref[:, pl.ds(pl.multiple_of(me * 128, 128), 128)]
    dpf[...] = jnp.zeros_like(dpf)

    loads[1].wait()

    def turn(at):
        span = pl.ds(pl.multiple_of(at * 256, 256), 256)
        tgrid[:, span] = grid_v[span, :].T
    blocks(4, turn)
    loads[2].wait()

    def make_query(at):
        span = pl.ds(pl.multiple_of(at * 256, 256), 256)
        qt[:, span] = dot(wq_v[...], tgrid[:, span]).astype(BF16)
    blocks(4, make_query)

    loads[3].wait()
    for copy in halos:
        copy.wait()

    def make_table(at):
        span = pl.ds(pl.multiple_of(at * 512, 512), 512)
        tkv[span, :] = dot(wkv_v[span, :], th[...], NT).astype(BF16)
    blocks(4, make_table)
    for e in range(3):
        def gather(at, e=e):
            span = pl.ds(pl.multiple_of(at * 512, 512), 512)
            kvg[e, span, :] = dot(tkv[span, :], oht[e], NT).astype(BF16)
        blocks(4, gather)
    loads[4].wait()

    def send_pred(target):
        return remote(
            preds.at[target], predr.at[me], ps_s.at[target], ps_r.at[me], (target, mp)
        )

    def tile(at):
        lanes = pl.ds(pl.multiple_of(at * LANES, LANES), LANES)

        def head(h):
            rows = pl.ds(pl.multiple_of(h * 64, 64), 64)
            vrows = pl.ds(pl.multiple_of(1024 + h * 64, 64), 64)
            query = qt[rows, lanes].astype(F32)
            raised = []
            for e in range(3):
                key = kvg[e, rows, lanes].astype(F32)
                raised.append(jnp.exp(jnp.sum(query * key, axis=0, keepdims=True) * 0.125))
            total = raised[0] + raised[1] + raised[2]
            out = None
            for e in range(3):
                weight = raised[e] / total
                wts[h, e:e + 1, lanes] = weight
                term = weight.astype(BF16).astype(F32) * kvg[e, vrows, lanes].astype(F32)
                out = term if out is None else out + term
            att[rows, lanes] = out.astype(BF16)
        blocks(16, head)
        mixed = (tgrid[:, lanes].astype(F32) + dot(wo_v[...], att[:, lanes])).astype(BF16)
        mix[:, lanes] = mixed
        pred = dot(wfp[pl.ds(0, FIELD_ROWS), :], mixed)
        for half in range(2):
            target = 2 * at + half
            preds[target] = pred[:, 128 * half:128 * half + 128]

            @pl.when(target != me)
            def _():
                send_pred(target).start()

            @pl.when(target == me)
            def _():
                predr[me] = pred[:, 128 * half:128 * half + 128]
    blocks(4, tile)

    def turn_out(at):
        span = pl.ds(pl.multiple_of(at * 256, 256), 256)
        wot_v[:, span] = wo_v[span, :].T
    blocks(4, turn_out)

    for by in range(1, 8):
        source = member_peer(by)
        remote(preds.at[source], predr.at[source], ps_s.at[source], ps_r.at[source],
               (source, mp)).wait()
    fair = (1.0 - (1.0 - ALPHA_FAIR) / MEMBERS) / (MEMBERS * (MEMBERS - 1))
    area = area_ref[:, pl.ds(pl.multiple_of(me * 128, 128), 128)]

    def crps(at):
        rows = pl.ds(pl.multiple_of(at * 16, 16), 16)
        truth = tpad[rows, :]
        scale = field_ref[rows, :] * area
        pred = [predr[m, rows, :] for m in range(MEMBERS)]
        spread = [jnp.zeros((16, 128), F32) for _ in range(MEMBERS)]
        for i in range(MEMBERS):
            for j in range(i + 1, MEMBERS):
                term = soft_sign(pred[i] - pred[j])
                spread[i] = spread[i] + term
                spread[j] = spread[j] - term
        for m in range(MEMBERS):
            dps[m, rows, :] = (
                scale * (soft_sign(pred[m] - truth) * (1.0 / MEMBERS) - fair * spread[m])
            ).astype(BF16)
    blocks(FIELD_ROWS // 16, crps)
    d_copies = []
    for by in range(1, 8):
        target = member_peer(by)
        copy = remote(dps.at[target], dpr.at[me], dp_s.at[by], dp_r.at[me], (target, mp))
        copy.start()
        d_copies.append(copy)
    dpr[me] = dps[me]
    for by in range(1, 8):
        source = member_peer(by)
        remote(dps.at[source], dpr.at[source], dp_s.at[by], dp_r.at[source],
               (source, mp)).wait_recv()
    for copy in d_copies:
        copy.wait_send()
    for j in range(MEMBERS):
        dpf[pl.ds(0, FIELD_ROWS), 128 * j:128 * j + 128] = dpr[j]

    dmix = tgrid

    def make_dmix(at):
        span = pl.ds(pl.multiple_of(at * 256, 256), 256)
        dmix[span, :] = dot(wft[span, :], dpf[...]).astype(BF16)
    blocks(4, make_dmix)

    def halves(half, peer):
        return y_peer(peer) if half == 0 else z_peer(peer)

    def store_unit(ref, unit, value, paired):
        if paired:
            value = value.reshape(2, 16, 8, 512).transpose(1, 0, 2, 3).reshape(256, 512)
        ref[0, unit] = value[:, :256].astype(BF16)
        second = value[:, 256:].reshape(4, 4, 16, 256).transpose(1, 0, 2, 3).reshape(256, 256)
        ref[1, unit] = second.astype(BF16)

    units = [4, 3, 3, 3, 3]
    sets = [(send_buf, recv_buf.at[0], w_own, w_r1, w_s1, w_r2, w_fin)] + [
        (send_buf.at[:, pl.ds(0, 3)], recv_buf.at[n % 2, :, pl.ds(0, 3)])
        + tuple(ref.at[n - 1] for ref in (h_own, h_r1, h_s1, h_r2, h_fin))
        for n in range(1, 5)
    ]

    def core_copy(n):
        return remote(sets[n][0], sets[n][1], core_s.at[n], core_r.at[n], sibling)

    def one_copy(n, half, by):
        first = lax.rem((y if half == 0 else z) + by, 4)
        return remote(
            sets[n][2].at[half, :, pl.ds(pl.multiple_of(first * 64, 64), 64), :],
            sets[n][3].at[half, by - 1],
            one_s.at[n, half, by - 1], one_r.at[n, half, by - 1], halves(half, by),
        )

    def two_copy(n, half, by):
        second = lax.rem((z if half == 0 else y) + by, 4)
        return remote(
            sets[n][4].at[half, :, pl.ds(pl.multiple_of(second * 16, 16), 16), :],
            sets[n][5].at[half, by - 1],
            two_s.at[n, half, by - 1], two_r.at[n, half, by - 1], halves(1 - half, by),
        )

    def start_one(n):
        core_copy(n).wait()
        own, recv = sets[n][2], sets[n][1]
        for half in range(2):
            def add(unit, half=half):
                own[half, unit] = (
                    own[half, unit].astype(F32) + recv[half, unit].astype(F32)
                ).astype(BF16)
            blocks(units[n], add)
            for by in (2, 1, 3):
                one_copy(n, half, by).start()

    def start_two(n):
        for half in range(2):
            for by in (1, 3, 2):
                one_copy(n, half, by).wait()
            first = pl.ds(pl.multiple_of((y if half == 0 else z) * 64, 64), 64)
            own, r1, s1 = sets[n][2], sets[n][3], sets[n][4]
            for unit in range(units[n]):
                total = own[half, unit, first, :].astype(F32)
                for slot in range(3):
                    total = total + r1[half, slot, unit].astype(F32)
                s1[half, unit] = total.astype(BF16)
            for by in (2, 1, 3):
                two_copy(n, half, by).start()

    def x_targets(n):
        if n == 0:
            return [(0, i, 2 * i + k) for i in range(4) for k in range(2)]
        j = lax.rem(x + n, 4)
        return [(1, 0, 2 * j), (1, 0, 2 * j + 1), (2, 1, j), (2, 2, 4 + j)]

    def x_copy(n, index, kind, unit, target):
        return remote(
            sets[n][6].at[unit], rx.at[kind, me], x_s.at[n, index], x_r.at[kind, me],
            (target, mp),
        )

    def start_x(n):
        fin, s1, r2 = sets[n][6], sets[n][4], sets[n][5]
        for half in range(2):
            for by in (1, 3, 2):
                two_copy(n, half, by).wait()
            second = pl.ds(pl.multiple_of((z if half == 0 else y) * 16, 16), 16)
            for unit in range(units[n]):
                total = s1[half, unit, second, :].astype(F32)
                for slot in range(3):
                    total = total + r2[half, slot, unit].astype(F32)
                fin[unit, :, 256 * half:256 * half + 256] = total.astype(BF16)
        for index, (kind, unit, target) in enumerate(x_targets(n)):
            @pl.when(target != me)
            def _():
                x_copy(n, index, kind, unit, target).start()

            @pl.when(target == me)
            def _():
                rx[kind, me] = fin[unit]

    def end_x(n):
        for index, (kind, unit, target) in enumerate(x_targets(n)):
            @pl.when(target != me)
            def _():
                x_copy(n, index, kind, unit, target).wait_send()

    own_cols = pl.ds(pl.multiple_of(c * 512, 512), 512)
    other_cols = pl.ds(pl.multiple_of(other * 512, 512), 512)

    for target_ref, cols in ((send_buf, other_cols), (w_own, own_cols)):
        def out_unit(unit):
            span = pl.ds(pl.multiple_of(unit * 256, 256), 256)
            store_unit(target_ref, unit, dot(dmix[span, :], att[cols, :], NT), True)
        blocks(4, out_unit)
        if target_ref is send_buf:
            core_copy(0).start()

    g_fields = dot(dpf[pl.ds(0, FIELD_ROWS), :], mix[...], NT)
    for j in range(MEMBERS):
        fs[j] = g_fields[:, 128 * j:128 * j + 128].astype(BF16)

    def f1_copy(by):
        target = member_peer(by)
        return remote(fs.at[target], fr1.at[me], f1_s.at[by], f1_r.at[me], (target, mp))

    for by in range(1, 8):
        f1_copy(by).start()
    fr1[me] = fs[me]
    start_one(0)

    def f2_copy(by):
        return remote(fr2.at[y], fr2.at[y], f2_s.at[by], f2_r.at[y], y_peer(by))

    def f3_copy(by):
        return remote(fr3.at[z], fr3.at[z], f3_s.at[by], f3_r.at[z], z_peer(by))

    def f4_copy(by):
        return remote(fr4.at[me], fr4.at[me], f4_s.at[by], f4_r.at[me], (member_peer(by), mp))

    def slots_sum(ref, count):
        total = ref[0].astype(F32)
        for slot in range(1, count):
            total = total + ref[slot].astype(F32)
        return total

    def start_f2():
        for by in range(1, 8):
            source = member_peer(by)
            remote(fs.at[source], fr1.at[source], f1_s.at[by], f1_r.at[source],
                   (source, mp)).wait_recv()
            f1_copy(by).wait_send()
        fr2[y] = slots_sum(fr1, 8).astype(BF16)
        for by in range(1, 4):
            f2_copy(by).start()

    def start_f3():
        for by in range(1, 4):
            source = lax.rem(y + by, 4)
            remote(fr2.at[source], fr2.at[source], f2_s.at[by], f2_r.at[source],
                   y_peer(by)).wait_recv()
            f2_copy(by).wait_send()
        fr3[z] = slots_sum(fr2, 4).astype(BF16)
        for by in range(1, 4):
            f3_copy(by).start()

    def start_f4():
        for by in range(1, 4):
            source = lax.rem(z + by, 4)
            remote(fr3.at[source], fr3.at[source], f3_s.at[by], f3_r.at[source],
                   z_peer(by)).wait_recv()
            f3_copy(by).wait_send()
        fr4[me] = (slots_sum(fr3, 4) * norm).astype(BF16)
        for by in range(1, 8):
            f4_copy(by).start()

    def end_f4():
        for by in range(1, 8):
            source = member_peer(by)
            remote(fr4.at[source], fr4.at[source], f4_s.at[by], f4_r.at[source],
                   (source, mp)).wait_recv()
            f4_copy(by).wait_send()
        for j in range(MEMBERS):
            gf_ref[:, 128 * j:128 * j + 128] = fr4[j, pl.ds(0, 100), :].astype(F32)

    dq, dret, tgt_t = mix, outgo, tkv
    dkv = (wo_v.at[pl.ds(0, 512)], wo_v.at[pl.ds(512, 512)], dkv_last)

    def attend_back(j):
        base = pl.multiple_of(j * 256, 256)
        datt[...] = dot(wot_v[pl.ds(base, 256), :], dmix[...])

        def head(at):
            hh = lax.div(at, 1024 // LANES)
            lanes = pl.ds(pl.multiple_of(lax.rem(at, 1024 // LANES) * LANES, LANES), LANES)
            local = pl.ds(pl.multiple_of(hh * 64, 64), 64)
            vlocal = pl.ds(pl.multiple_of(256 + hh * 64, 64), 64)
            rows = pl.ds(pl.multiple_of(base + hh * 64, 64), 64)
            vrows = pl.ds(pl.multiple_of(1024 + base + hh * 64, 64), 64)
            grad = datt[local, lanes]
            query = qt[rows, lanes].astype(F32)
            weight = [wts[4 * j + hh, e:e + 1, lanes] for e in range(3)]
            d_weight = [
                jnp.sum(grad * kvg[e, vrows, lanes].astype(F32), axis=0, keepdims=True)
                for e in range(3)
            ]
            inner = weight[0] * d_weight[0] + weight[1] * d_weight[1] + weight[2] * d_weight[2]
            out = None
            for e in range(3):
                d_score = weight[e] * (d_weight[e] - inner) * 0.125
                term = d_score * kvg[e, rows, lanes].astype(F32)
                out = term if out is None else out + term
                dkv[e][local, lanes] = (d_score * query).astype(BF16)
                dkv[e][vlocal, lanes] = (weight[e].astype(BF16).astype(F32) * grad).astype(BF16)
            dq[rows, lanes] = out.astype(BF16)
        blocks(4 * (1024 // LANES), head)

    def gradients(n, j):
        base = pl.multiple_of(j * 256, 256)
        spans = (pl.ds(base, 256), pl.ds(pl.multiple_of(1024 + base, 256), 256))
        for which, span in enumerate(spans):
            rows = pl.ds(256 * which, 256)
            total = dot(dkv[0][rows, :], oht[0])
            for e in range(1, 3):
                total = total + dot(dkv[e][rows, :], oht[e])
            tgt_t[span, :] = total.astype(BF16)
        for target_ref, cols in ((sets[n][0], other_cols), (sets[n][2], own_cols)):
            store_unit(target_ref, 0, dot(dq[spans[0], :], grid_v[:, cols]), True)
            for which, span in enumerate(spans):
                store_unit(target_ref, 1 + which, dot(tgt_t[span, :], th[:, cols]), False)
            if target_ref is sets[n][0]:
                core_copy(n).start()

    background = {
        1: (start_f2, lambda: start_two(0)),
        2: (start_f3, lambda: start_one(1), lambda: start_x(0)),
        3: (start_f4, lambda: start_two(1), lambda: start_one(2)),
        4: (lambda: start_x(1), lambda: start_two(2), lambda: start_one(3)),
    }
    for n in range(1, 5):
        j = lax.rem(x + n, 4)
        attend_back(j)
        for task in background[n]:
            task()
        gradients(n, j)

    table = tgt_t[...].T
    dret[...] = dot(table[128:], wkv_v[...]).astype(BF16)

    def back_copy(r):
        return remote(
            dret.at[pl.ds(32 * r, 32)], drecv.at[pl.ds(32 * (3 - r), 32)],
            back_s.at[r], back_r.at[3 - r], halo_peer(OFFSETS[r]),
        )

    for r in range(4):
        back_copy(r).start()
    start_one(4)
    start_x(2)
    start_two(3)
    own_hidden = dot(table[:128], wkv_v[...])

    stage = att

    def out_copy(at):
        span = pl.ds(pl.multiple_of(at * 256, 256), 256)
        return pltpu.make_async_copy(stage.at[span], dgrid_hbm.at[span], out_sem.at[at])

    def grid_grad(at):
        span = pl.ds(pl.multiple_of(at * 256, 256), 256)
        through = dot(dq[:, span].T, wq_v[...])
        direct = dot(dpf[:, span].T, wfp[...]).astype(BF16).astype(F32)
        stage[span, :] = (direct + through).astype(BF16)
        out_copy(at).start()

    grid_grad(0)
    start_two(4)
    start_x(3)
    blocks(3, lambda at: grid_grad(at + 1))
    for r in range(4):
        back_copy(r).wait()
    dhid_ref[...] = (own_hidden + dot(halo_hot.T, drecv[...])).astype(BF16)
    start_x(4)
    end_f4()
    for n in range(5):
        end_x(n)
    for kind in range(3):
        for by in range(1, 8):
            source = member_peer(by)
            remote(rx.at[kind, source], rx.at[kind, source], x_s.at[0, 0],
                   x_r.at[kind, source], (source, mp)).wait_recv()

    def member_sum(kind, half):
        total = rx[kind, half].astype(F32)
        for other_x in range(1, 4):
            total = total + rx[kind, 2 * other_x + half].astype(F32)
        return total * norm

    for half in range(2):
        cols = slice(512 * half, 512 * half + 512)
        for kind, ref in ((0, go_ref), (1, gq_ref)):
            total = member_sum(kind, half)
            ref[:, cols] = jnp.where(c == 0, total[:8], total[8:])
        gkv_ref[:, cols] = member_sum(2, half)
    for at in range(4):
        out_copy(at).wait()


def on_device(
    hidden, grid_emb, targets, area_w, field_w, edge_table, halo_rows,
    w_query, w_keyval, w_attn_out, w_fields,
):
    def vm(*shape, dtype=BF16):
        return pltpu.VMEM(shape, dtype)

    def sems(*shape):
        return pltpu.SemaphoreType.DMA(shape)

    def comm(lead, count):
        return [
            vm(*lead, 2, count, 256, 256), vm(*lead, 2, 3, count, 64, 256),
            vm(*lead, 2, count, 64, 256), vm(*lead, 2, 3, count, 16, 256),
            vm(*lead, count, 16, 512),
        ]

    square = (1024, 1024)
    scratch = [
        vm(*square), vm(*square), vm(2048, 1024), vm(*square), vm(*square),
        vm(*square), vm(*square), vm(*square), vm(*square),
        vm(256, 1024), vm(2048, 256), vm(3, 1024, 256), vm(3, 2048, 1024),
        vm(16, 8, 1024, dtype=F32),
        vm(128, 1024), vm(1024, 128), vm(FIELD_ROWS, 128, dtype=F32),
        vm(8, FIELD_ROWS, 128, dtype=F32), vm(8, FIELD_ROWS, 128, dtype=F32),
        vm(8, FIELD_ROWS, 128), vm(8, FIELD_ROWS, 128), vm(128, 1024),
        vm(256, 1024, dtype=F32), vm(512, 1024),
        vm(128, 1024), vm(128, 1024),
        vm(8, FIELD_ROWS, 128), vm(8, FIELD_ROWS, 128), vm(4, FIELD_ROWS, 128),
        vm(4, FIELD_ROWS, 128), vm(8, FIELD_ROWS, 128),
        vm(2, 4, 256, 256), vm(2, 2, 4, 256, 256), *comm((), 4), *comm((4,), 3),
        vm(3, 8, 16, 512),
        sems(5), sems(4), sems(4), sems(8), sems(8), sems(8), sems(8), sems(4), sems(4),
        sems(8), sems(8), sems(4), sems(4), sems(4), sems(4), sems(8), sems(8),
        sems(5), sems(5), sems(5, 2, 3), sems(5, 2, 3), sems(5, 2, 3), sems(5, 2, 3),
        sems(5, 8), sems(3, 8), sems(4),
    ]
    vmem = pl.BlockSpec(memory_space=pltpu.VMEM)
    hbm = pl.BlockSpec(memory_space=pl.ANY)
    outs = pl.pallas_call(
        kernel,
        out_shape=(
            jax.ShapeDtypeStruct((128, 1024), BF16),
            jax.ShapeDtypeStruct(square, BF16),
            jax.ShapeDtypeStruct((8, 1024), F32),
            jax.ShapeDtypeStruct((16, 1024), F32),
            jax.ShapeDtypeStruct((8, 1024), F32),
            jax.ShapeDtypeStruct((100, 1024), F32),
        ),
        in_specs=[hbm, hbm, vmem, vmem, vmem, vmem, vmem, hbm, hbm, hbm, vmem],
        out_specs=(vmem, hbm, vmem, vmem, vmem, vmem),
        scratch_shapes=scratch,
        compiler_params=pltpu.CompilerParams(
            collective_id=0, has_side_effects=True, vmem_limit_bytes=63 * 1024 * 1024
        ),
        cost_estimate=pl.CostEstimate(
            flops=22_000_000_000, bytes_accessed=16_000_000, transcendentals=500_000
        ),
        name="decoder_backward",
    )(
        hidden[0], grid_emb[0], targets, area_w.reshape(1, 1024),
        jnp.pad(field_w, (0, FIELD_ROWS - 100)).reshape(FIELD_ROWS, 1),
        edge_table, halo_rows.reshape(128, 1),
        w_query, w_keyval, w_attn_out, w_fields,
    )
    return (outs[0][None], outs[1][None], *outs[2:])


def solution(mesh):
    in_specs = (
        P("member", "mp", None),
        P("member", "mp", None),
        P(None, "mp"),
        P("mp"),
        P(),
        P("mp", None),
        P("mp", None),
        P(),
        P(),
        P(),
        P(),
    )
    out_specs = (
        P("member", "mp", None),
        P("member", "mp", None),
        P(("member", "mp"), None),
        P(("member", "mp"), None),
        P(("member", "mp"), None),
        P(),
    )
    return jax.shard_map(
        on_device, mesh=mesh, in_specs=in_specs, out_specs=out_specs, check_vma=False
    )
```

time: 2280 us -> 116 us (0.05); the launches traced: 2240 us -> 116 us
  waiting for transfers between devices: 1860 us -> 0 us
  local copies, waits for them, and re-layouts: 167 us -> 12 us
  other arithmetic: 130 us -> 0 us
  Pallas kernels: 0 us -> 103 us
  matrix products: 47.5 us -> 0 us
    reduce_scatter x3 -> x0, waiting for transfers between devices: 1820 us -> none  [the longest x1 646 us: on_device(): lax.psum_scatter(keyval_terms, ('member', 'mp'), scatter_dimension=0, til...]
    pallas_call x0 -> x1, Pallas kernels: none -> 103 us  [on_device(): pl.pallas_call(kernel, out_shape=(jax.ShapeDtypeStruct((128, 1024), BF16)...]
    scatter-add x3 -> x0, other arithmetic: 59.1 us -> none  [the longest x1 28.6 us: on_device(): jax.ops.segment_sum(d_keys.reshape(grid_count * edges_each, width), flat_...]
    gather x3 -> x0, local copies, waits for them, and re-layouts: 49.8 us -> none  [the longest x2 48.8 us: on_device(): picked = table[edge_table]]
    dot_general x12 -> x0, matrix products: 47.5 us -> none  [product(): lax.dot_general(left, right, numbers, preferred_element_type=jnp.float32)]
    all_gather x1 -> x0, waiting for transfers between devices: 29.4 us -> none  [on_device(): ensemble = lax.all_gather(predicted[None], 'member', axis=0, tiled=True)]
    unnamed x45 -> x15, local copies, waits for them, and re-layouts: 36.9 us -> 9.17 us
  transfers between devices with their start and end apart: 13 -> 0, of which waited for: 7 -> 0; matrix products, arithmetic and copies ran while one was open for 9% -> 0% of each run, Pallas kernels for 0% -> 0%
where the time goes in v1:
time: 116 us
  Pallas kernels  103 us (89%)
  local copies, waits for them, and re-layouts  12 us (10%)
    pallas_call x1, Pallas kernels, on_device(): pl.pallas_call(kernel, out_shape=(jax.ShapeDtypeStruct((128, 1024), BF16)...  103 us
    unnamed x15, local copies, waits for them, and re-layouts  9.17 us

profile of v1, /device:TPU:1, one launch (start us, length us, event | category | flops | bytes accessed | tf_op | source)
XLA Modules:
  0.0 115.7 jit_solution(3522522602978820926)
XLA Ops:
  0.6 0.7 pad_bitcast_fusion
  1.3 0.7 copy.17.field_ref
  2.0 1.4 %reshape.24.halo_ref = s32[128,1]{1,0:T(8,128)} reshape(s32[4,32]{1,0:T(4,128)} %param.17) | data formatting | bytes 1024 | tf_op jit(solution)/shard_map/reshape | solution.py:615
  3.4 1.7 %copy.18.edge_ref = s32[1024,3]{1,0:T(8,128)} copy(s32[1024,3]{0,1:T(4,128)} %param.16) | data formatting | bytes 24576 | tf_op args[5]
  5.2 103.1 %decoder_backward.1 = (bf16[128,1024]{1,0:T(8,128)(2,1)}, bf16[1024,1024]{1,0:T(8,128)(2,1)}, f32[8,1024]{1,0:T(8,128)}, f32[16,1024]{1,0:T(8,128)}, f32[8,1024]{1,0:T(8,128)}, /*index=5*/f32[100,1024]{1,0:T(8,128)}) custom-call(bf16[128,1024]{1,0:T(8,128)(2,1)} %bitcast.10, bf16[1024,1024]{1,0:T(8,128)(2,1)} %bitcast.9, f32[100,1024]{1,0:T(8,128)} %tgt_ref.1, ...), custom_call_target="tpu_custom_call" | custom-call | flops 22000001024 | bytes 16000000 | tf_op jit(solution)/shard_map/decoder_backward/pallas_call | solution.py:592
  108.3 1.7 %copy.26 = bf16[1,128,1024]{2,1,0:T(8,128)(2,1)} copy(bf16[1,128,1024]{2,1,0:T(8,128)(2,1)} %bitcast.8) | data formatting | bytes 524288
  110.0 0.0 copy-start.3
  110.0 0.0 copy-start.1
  110.0 0.0 copy-start.2
  110.0 0.0 copy-start
  110.0 3.1 %copy.27 = bf16[1,1024,1024]{2,1,0:T(8,128)(2,1)} copy(bf16[1,1024,1024]{2,1,0:T(8,128)(2,1)} %bitcast.7) | data formatting | bytes 4194304
  113.1 0.0 copy-done.3
  113.1 0.6 copy.28
  113.7 0.0 copy-done.1
  113.7 0.6 copy.29
  114.4 0.0 copy-done.2
  114.4 0.6 copy.30
  115.0 0.0 copy-done
  115.0 0.8 copy.31
Async XLA Ops:
  110.0 3.2 %copy-start.3 = (f32[8,1024]{1,0:T(8,128)S(1)}, f32[8,1024]{1,0:T(8,128)}, u32[]{:S(2)}) copy-start(f32[8,1024]{1,0:T(8,128)} %get-tuple-element.26) | copy-start | bytes 98308
  110.0 3.8 %copy-start.1 = (f32[16,1024]{1,0:T(8,128)S(1)}, f32[16,1024]{1,0:T(8,128)}, u32[]{:S(2)}) copy-start(f32[16,1024]{1,0:T(8,128)} %get-tuple-element.27) | copy-start | bytes 196612
  110.0 4.4 %copy-start.2 = (f32[8,1024]{1,0:T(8,128)S(1)}, f32[8,1024]{1,0:T(8,128)}, u32[]{:S(2)}) copy-start(f32[8,1024]{1,0:T(8,128)} %get-tuple-element.28) | copy-start | bytes 98308
  110.0 5.0 %copy-start = (f32[100,1024]{1,0:T(8,128)S(1)}, f32[100,1024]{1,0:T(8,128)}, u32[]{:S(2)}) copy-start(f32[100,1024]{1,0:T(8,128)} %get-tuple-element.29) | copy-start | bytes 1228804

commit v2 on v1

v2 whole, which is shorter than its diff:
```python
import math

import jax
import jax.numpy as jnp
from jax import lax
from jax.experimental import pallas as pl
from jax.experimental.pallas import tpu as pltpu
from jax.sharding import PartitionSpec as P

ALPHA_FAIR = 0.95
KAPPA = 0.1
OFFSETS = (-2, -1, 1, 2)
MEMBERS = 8
FIELD_ROWS = 112
TILE = 512
MESH = pl.DeviceIdType.MESH
BF16 = jnp.bfloat16
F32 = jnp.float32
NT = (((1,), (1,)), ((), ()))
NN = (((1,), (0,)), ((), ()))


def dot(left, right, numbers=NN):
    return lax.dot_general(left, right, numbers, preferred_element_type=F32)


def soft_sign(value):
    return value * lax.rsqrt(value * value + KAPPA * KAPPA)


def blocks(count, body, unroll=1):
    def step(at, carry):
        body(at)
        return carry

    lax.fori_loop(0, count, step, 0, unroll=unroll)


def part(at, size, base=0):
    return pl.ds(pl.multiple_of(base + at * size, size), size)


def kernel(
    hid_hbm, grid_hbm, tgt_ref, area_ref, field_ref, edge_ref, halo_ref,
    wq_hbm, wkv_hbm, wo_hbm, wf_ref,
    dhid_ref, dgrid_hbm, gq_ref, gkv_ref, go_ref, gf_ref,
    grid_v, wq_v, wkv_v, wo_v, wot_v, tgrid, qt, att, mix, th, tkv, oh, kvg, wts,
    wfp, wft, frow, fcol, tpad, preds, predr, dps, dpf,
    datt, dkv_last, outgo, hall, dq,
    drecv, dkfull, kvr, kvh, direct,
    fs, fr1, fr2, fr3, fr4,
    w_g, w_recv, w_r1, w_s1, w_r2, w_fin,
    h_g, h_recv, h_r1, h_s1, h_r2, h_fin,
    k_own, k_r1, k_s1, k_r2,
    rx,
    load_sem, halo_s, halo_r, all_s, all_r, ps_s, ps_r, dp_s, dp_r, back_s, back_r, kv_s, kv_r,
    kvh_s, kvh_r, direct_s, direct_r,
    f1_s, f1_r, f2_s, f2_r, f3_s, f3_r, f4_s, f4_r,
    core_s, core_r, one_s, one_r, two_s, two_r, x_s, x_r, out_sem,
):
    me = lax.axis_index("member")
    mp = lax.axis_index("mp")
    x, c = lax.div(me, 2), lax.rem(me, 2)
    y, z = lax.div(mp, 4), lax.rem(mp, 4)
    other = 1 - c
    sibling = (2 * x + other, mp)
    norm = 1.0 / math.sqrt(MEMBERS * 16384.0)

    def halo_peer(by):
        return (me, lax.rem(mp + by + 16, 16))

    def member_peer(by):
        return lax.rem(me + by, 8)

    def x_peer(by):
        return 2 * lax.rem(x + by, 4) + c

    def y_peer(by):
        return (me, 4 * lax.rem(y + by, 4) + z)

    def z_peer(by):
        return (me, 4 * y + lax.rem(z + by, 4))

    def remote(src, dst, send, recv, device):
        return pltpu.make_async_remote_copy(
            src_ref=src, dst_ref=dst, send_sem=send, recv_sem=recv,
            device_id=device, device_id_type=MESH,
        )

    loads = [
        pltpu.make_async_copy(src, dst, load_sem.at[n])
        for n, (src, dst) in enumerate((
            (hid_hbm, th.at[pl.ds(0, 128)]), (grid_hbm, grid_v), (wq_hbm, wq_v),
            (wkv_hbm, wkv_v), (wo_hbm, wo_v), (hid_hbm, hall.at[part(me, 128)]),
        ))
    ]
    for load in loads:
        load.start()
    barrier = pltpu.get_barrier_semaphore()
    partners = (
        [(me, lax.rem(mp + by, 16)) for by in range(1, 16)]
        + [(member_peer(by), mp) for by in range(1, 8)]
        + [(member_peer(by), halo_peer(far)[1]) for by in range(1, 8) for far in OFFSETS]
    )
    for partner in partners:
        pl.semaphore_signal(barrier, inc=1, device_id=partner, device_id_type=MESH)

    for e in range(3):
        oh[e] = (
            lax.broadcasted_iota(jnp.int32, (256, 1024), 0) == edge_ref[e:e + 1, :]
        ).astype(BF16)
    wfp[...] = jnp.zeros_like(wfp)
    wfp[pl.ds(0, 100), :] = wf_ref[...]
    wft[...] = wfp[...].T
    tpad[...] = jnp.zeros_like(tpad)
    tpad[pl.ds(0, 100), :] = tgt_ref[...]
    frow[...] = jnp.zeros_like(frow)
    frow[pl.ds(0, 1), pl.ds(0, 100)] = field_ref[...]
    fcol[...] = jnp.broadcast_to(frow[pl.ds(0, 1), :], (128, 128)).T

    halo_row = jnp.concatenate([halo_ref[l:l + 1, :] for l in range(4)], axis=1)
    halo_home = (
        lax.broadcasted_iota(jnp.int32, (128, 128), 0) == halo_row
    ).astype(BF16)
    loads[0].wait()
    outgo[...] = dot(halo_home.T, th[pl.ds(0, 128), :]).astype(BF16)
    pl.semaphore_wait(barrier, len(partners))
    halos = []
    for l, by in enumerate(OFFSETS):
        copy = remote(
            outgo.at[pl.ds(32 * l, 32)], th.at[pl.ds(128 + 32 * (3 - l), 32)],
            halo_s.at[l], halo_r.at[3 - l], halo_peer(by),
        )
        copy.start()
        halos.append(copy)

    def share(source, at, device):
        return remote(
            hall.at[part(source, 128)] if at > 3 else th.at[pl.ds(0, 128)],
            hall.at[part(source, 128)], all_s.at[at], all_r.at[source], device,
        )

    for by in (1, 3, 2):
        share(me, by, (x_peer(by), mp)).start()
    share(me, 0, sibling).start()

    loads[1].wait()

    def turn(at):
        tgrid[:, part(at, 256)] = grid_v[part(at, 256), :].T
    blocks(4, turn)
    loads[2].wait()
    for at in range(2):
        lanes = pl.ds(TILE * at, TILE)
        qt[:, lanes] = dot(wq_v[...], tgrid[:, lanes]).astype(BF16)

    loads[3].wait()
    for copy in halos:
        copy.wait()

    def make_table(at):
        tkv[part(at, 512), :] = dot(wkv_v[part(at, 512), :], th[...], NT).astype(BF16)
    blocks(4, make_table)

    def gather(t):
        lanes = pl.ds(t * TILE, TILE)
        for e in range(3):
            def rows_of(at, e=e):
                kvg[e, part(at, 512), lanes] = dot(
                    tkv[part(at, 512), :], oh[e, :, lanes]
                ).astype(BF16)
            blocks(4, rows_of)

    def attend(t):
        lanes = pl.ds(t * TILE, TILE)

        def head(h):
            rows, vrows = part(h, 64), part(h, 64, 1024)
            query = qt[rows, lanes].astype(F32)
            raised = []
            for e in range(3):
                key = kvg[e, rows, lanes].astype(F32)
                raised.append(jnp.exp(jnp.sum(query * key, axis=0, keepdims=True) * 0.125))
            total = raised[0] + raised[1] + raised[2]
            out = None
            for e in range(3):
                weight = raised[e] / total
                wts[h, e:e + 1, lanes] = weight
                term = weight.astype(BF16).astype(F32) * kvg[e, vrows, lanes].astype(F32)
                out = term if out is None else out + term
            att[rows, lanes] = out.astype(BF16)
        blocks(16, head, 2)

    def pred_copy(t, by):
        target = member_peer(by)
        return remote(
            preds.at[t, part(target, 16)], predr.at[t, me], ps_s.at[t, by], ps_r.at[t, me],
            (target, mp),
        )

    def predict(t):
        lanes = pl.ds(t * TILE, TILE)
        mixed = (tgrid[:, lanes].astype(F32) + dot(wo_v[...], att[:, lanes])).astype(BF16)
        mix[:, lanes] = mixed
        preds[t] = dot(wfp[...], mixed)
        for by in range(1, 8):
            pred_copy(t, by).start()
        predr[t, me] = preds[t, part(me, 16), :]

    fair = (1.0 - (1.0 - ALPHA_FAIR) / MEMBERS) / (MEMBERS * (MEMBERS - 1))
    mine = part(me, 16)

    def dp_copy(t, by):
        target = member_peer(by)
        return remote(
            dps.at[t, target], dpf.at[mine, pl.ds(t * TILE, TILE)],
            dp_s.at[t, by], dp_r.at[t, me], (target, mp),
        )

    def crps(t):
        for by in range(1, 8):
            source = member_peer(by)
            remote(preds.at[t, part(source, 16)], predr.at[t, source], ps_s.at[t, by],
                   ps_r.at[t, source], (source, mp)).wait_recv()
            pred_copy(t, by).wait_send()
        for chunk in range(TILE // 128):
            lanes = pl.ds(128 * chunk, 128)
            points = pl.ds(t * TILE + 128 * chunk, 128)
            truth = tpad[mine, points]
            scale = fcol[mine, :] * area_ref[:, points]
            pred = [predr[t, m, :, lanes] for m in range(MEMBERS)]
            spread = [jnp.zeros((16, 128), F32) for _ in range(MEMBERS)]
            for i in range(MEMBERS):
                for j in range(i + 1, MEMBERS):
                    term = soft_sign(pred[i] - pred[j])
                    spread[i] = spread[i] + term
                    spread[j] = spread[j] - term
            for m in range(MEMBERS):
                dps[t, m, :, lanes] = (
                    scale * (soft_sign(pred[m] - truth) * (1.0 / MEMBERS) - fair * spread[m])
                ).astype(BF16)
        for by in range(1, 8):
            dp_copy(t, by).start()
        dpf[mine, pl.ds(t * TILE, TILE)] = dps[t, me]

    dmix = tgrid

    def make_dmix(t):
        lanes = pl.ds(t * TILE, TILE)
        for by in range(1, 8):
            source = member_peer(by)
            remote(dps.at[t, source], dpf.at[part(source, 16), lanes], dp_s.at[t, by],
                   dp_r.at[t, source], (source, mp)).wait_recv()
            dp_copy(t, by).wait_send()

        def rows_of(at):
            dmix[part(at, 512), lanes] = dot(wft[part(at, 512), :], dpf[:, lanes]).astype(BF16)
        blocks(2, rows_of)

    gather(0)
    loads[4].wait()
    attend(0)
    predict(0)
    gather(1)
    crps(0)
    attend(1)
    predict(1)

    def turn_out(at):
        wot_v[:, part(at, 256)] = wo_v[part(at, 256), :].T
    blocks(4, turn_out)
    for by in range(1, 4):
        source = x_peer(by)
        share(me, by, (x_peer(by), mp)).wait_send()
        share(source, 0, sibling).wait_recv()
        share(source, 3 + by, sibling).start()
    share(me, 0, sibling).wait_send()
    crps(1)

    dkv = (wo_v.at[pl.ds(0, 512)], wo_v.at[pl.ds(512, 512)], dkv_last)

    def block_of(n):
        return lax.rem(x + n, 4)

    def attend_back(n, tiles):
        j = block_of(n)
        base = pl.multiple_of(j * 256, 256)
        span = pl.ds(tiles[0] * TILE, len(tiles) * TILE)
        datt[:, span] = dot(wot_v[pl.ds(base, 256), :], dmix[:, span])
        for t in tiles:
            lanes = pl.ds(t * TILE, TILE)

            def head(hh):
                local, vlocal = part(hh, 64), part(hh, 64, 256)
                rows = pl.ds(pl.multiple_of(base + hh * 64, 64), 64)
                vrows = pl.ds(pl.multiple_of(1024 + base + hh * 64, 64), 64)
                grad = datt[local, lanes]
                query = qt[rows, lanes].astype(F32)
                weight = [wts[4 * j + hh, e:e + 1, lanes] for e in range(3)]
                d_weight = [
                    jnp.sum(grad * kvg[e, vrows, lanes].astype(F32), axis=0, keepdims=True)
                    for e in range(3)
                ]
                inner = (
                    weight[0] * d_weight[0] + weight[1] * d_weight[1] + weight[2] * d_weight[2]
                )
                out = None
                for e in range(3):
                    d_score = weight[e] * (d_weight[e] - inner) * 0.125
                    term = d_score * kvg[e, rows, lanes].astype(F32)
                    out = term if out is None else out + term
                    dkv[e][local, lanes] = (d_score * query).astype(BF16)
                    dkv[e][vlocal, lanes] = (
                        weight[e].astype(BF16).astype(F32) * grad
                    ).astype(BF16)
                dq[rows, lanes] = out.astype(BF16)
            blocks(4, head)

    def kv_targets(n):
        j = block_of(n)
        return (j, 4 + j)

    def kv_copy(n, which):
        target = kv_targets(n)[which]
        return remote(
            dkfull.at[pl.ds(0, 128), part(target, 256)], kvr.at[part(me, 128)],
            kv_s.at[n - 1, which], kv_r.at[me], (target, mp),
        )

    def kvh_copy(n, which, r):
        target = kv_targets(n)[which]
        return remote(
            dkfull.at[pl.ds(128 + 32 * r, 32), part(target, 256)],
            kvh.at[pl.ds(pl.multiple_of(me * 128 + 32 * (3 - r), 32), 32)],
            kvh_s.at[n - 1, which, r], kvh_r.at[me, 3 - r],
            (target, halo_peer(OFFSETS[r])[1]),
        )

    def scatter(n):
        total = dot(oh[0], dkv[0][...], NT)
        for e in range(1, 3):
            total = total + dot(oh[e], dkv[e][...], NT)
        for which in range(2):
            target = kv_targets(n)[which]
            piece = total[:, 256 * which:256 * which + 256].astype(BF16)
            dkfull[:, part(target, 256)] = piece

            @pl.when(target != me)
            def _():
                kv_copy(n, which).start()

            @pl.when(target == me)
            def _():
                kvr[part(me, 128), :] = piece[:128]

            for r in range(4):
                kvh_copy(n, which, r).start()

    def wait_keyval():
        for by in range(1, 8):
            source = member_peer(by)
            remote(kvr.at[part(source, 128)], kvr.at[part(source, 128)], kv_s.at[0, 0],
                   kv_r.at[source], (source, mp)).wait_recv()
        for source in range(MEMBERS):
            for r in range(4):
                rows = pl.ds(source * 128 + 32 * r, 32)
                remote(kvh.at[rows], kvh.at[rows], kvh_s.at[0, 0, r], kvh_r.at[source, r],
                       halo_peer(OFFSETS[r])).wait_recv()

    def end_keyval():
        for n in range(1, 5):
            for which in range(2):
                @pl.when(kv_targets(n)[which] != me)
                def _():
                    kv_copy(n, which).wait_send()

                for r in range(4):
                    kvh_copy(n, which, r).wait_send()

    def ring(half, by):
        return y_peer(by) if half == 0 else z_peer(by)

    def store_unit(ref, unit, value, crossed=True):
        for core in range(2):
            for half in range(2):
                at = 512 * core + 256 * half
                piece = value[:, at:at + 256].reshape(2, 4, 4, 8, 256)
                order = (2, 1, 0, 3, 4) if half == 1 and crossed else (1, 2, 0, 3, 4)
                ref[core, half, unit] = piece.transpose(order).reshape(256, 256).astype(BF16)

    units = [4, 1, 1, 1, 1, 1]
    sets = [(w_g, w_recv, w_g.at[c], w_r1, w_s1, w_r2, w_fin)] + [
        (h_g.at[n], h_recv.at[n], h_g.at[n, c], h_r1.at[n], h_s1.at[n], h_r2.at[n], h_fin.at[n])
        for n in range(4)
    ] + [(None, None, k_own, k_r1, k_s1, k_r2, None)]

    def core_copy(n):
        return remote(sets[n][0].at[other], sets[n][1], core_s.at[n], core_r.at[n], sibling)

    def one_copy(n, half, by):
        first = lax.rem((y if half == 0 else z) + by, 4)
        return remote(
            sets[n][2].at[half, :, part(first, 64), :], sets[n][3].at[half, by - 1],
            one_s.at[n, half, by - 1], one_r.at[n, half, by - 1], ring(half, by),
        )

    def two_copy(n, half, by):
        second = lax.rem((z if half == 0 else y) + by, 4)
        return remote(
            sets[n][4].at[half, :, part(second, 16), :], sets[n][5].at[half, by - 1],
            two_s.at[n, half, by - 1], two_r.at[n, half, by - 1], ring(1 - half, by),
        )

    def add_cores(n, half):
        own, recv = sets[n][2], sets[n][1]

        def add(unit):
            own[half, unit] = (
                own[half, unit].astype(F32) + recv[half, unit].astype(F32)
            ).astype(BF16)
        blocks(units[n], add)

    def start_one(n):
        core_copy(n).wait()
        for half in range(2):
            add_cores(n, half)
            for by in (2, 1, 3):
                one_copy(n, half, by).start()

    def direct_copy(by):
        target = lax.rem(mp + by, 16)
        return remote(
            sets[4][2].at[:, 0, part(target, 16), :], direct.at[by - 1],
            direct_s.at[by - 1], direct_r.at[by - 1], (me, target),
        )

    def start_direct():
        core_copy(4).wait()
        for half in range(2):
            add_cores(4, half)
        for by in (10, 6, 9, 7, 8, 5, 11, 2, 14, 3, 13, 1, 15, 4, 12):
            direct_copy(by).start()

    def end_direct():
        for by in range(1, 16):
            direct_copy(by).wait()
        for half in range(2):
            total = sets[4][2][half, 0, part(mp, 16), :].astype(F32)
            for by in range(1, 16):
                total = total + direct[by - 1, half].astype(F32)
            sets[4][6][0, :, 256 * half:256 * half + 256] = total.astype(BF16)
        send_x(4)

    def start_two(n):
        own, r1, s1 = sets[n][2], sets[n][3], sets[n][4]
        for half in range(2):
            for by in (1, 3, 2):
                one_copy(n, half, by).wait()
            first = part(y if half == 0 else z, 64)
            for unit in range(units[n]):
                total = own[half, unit, first, :].astype(F32)
                for slot in range(3):
                    total = total + r1[half, slot, unit].astype(F32)
                s1[half, unit] = total.astype(BF16)
            for by in (2, 1, 3):
                two_copy(n, half, by).start()

    def finish_two(n, half, unit):
        total = sets[n][4][half, unit, part(z if half == 0 else y, 16), :].astype(F32)
        for slot in range(3):
            total = total + sets[n][5][half, slot, unit].astype(F32)
        return total

    def x_targets(n):
        if n == 0:
            return [(0, i, 2 * i + k) for i in range(4) for k in range(2)]
        j = block_of(n)
        return [(1, 0, 2 * j), (1, 0, 2 * j + 1)]

    def x_copy(n, index, kind, unit, target):
        return remote(
            sets[n][6].at[unit], rx.at[kind, me], x_s.at[n, index], x_r.at[kind, me],
            (target, mp),
        )

    def start_x(n):
        fin = sets[n][6]
        for half in range(2):
            for by in (1, 3, 2):
                two_copy(n, half, by).wait()
            for unit in range(units[n]):
                fin[unit, :, 256 * half:256 * half + 256] = finish_two(n, half, unit).astype(BF16)
        send_x(n)

    def send_x(n):
        fin = sets[n][6]
        for index, (kind, unit, target) in enumerate(x_targets(n)):
            @pl.when(target != me)
            def _():
                x_copy(n, index, kind, unit, target).start()

            @pl.when(target == me)
            def _():
                rx[kind, me] = fin[unit]

    def end_x(n):
        for index, (kind, unit, target) in enumerate(x_targets(n)):
            @pl.when(target != me)
            def _():
                x_copy(n, index, kind, unit, target).wait_send()

    def query_grad(n):
        span = part(block_of(n), 256)
        store_unit(sets[n][0], 0, dot(dq[span, :], grid_v[...]), n < 4)
        core_copy(n).start()

    def f1_copy(by):
        target = member_peer(by)
        return remote(fs.at[target], fr1.at[me], f1_s.at[by], f1_r.at[me], (target, mp))

    def f2_copy(by):
        return remote(fr2.at[y], fr2.at[y], f2_s.at[by], f2_r.at[y], y_peer(by))

    def f3_copy(by):
        return remote(fr3.at[z], fr3.at[z], f3_s.at[by], f3_r.at[z], z_peer(by))

    def f4_copy(by):
        return remote(fr4.at[me], fr4.at[me], f4_s.at[by], f4_r.at[me], (member_peer(by), mp))

    def slots_sum(ref, count):
        total = ref[0].astype(F32)
        for slot in range(1, count):
            total = total + ref[slot].astype(F32)
        return total

    def start_f2():
        for by in range(1, 8):
            source = member_peer(by)
            remote(fs.at[source], fr1.at[source], f1_s.at[by], f1_r.at[source],
                   (source, mp)).wait_recv()
            f1_copy(by).wait_send()
        fr2[y] = slots_sum(fr1, 8).astype(BF16)
        for by in range(1, 4):
            f2_copy(by).start()

    def start_f3():
        for by in range(1, 4):
            source = lax.rem(y + by, 4)
            remote(fr2.at[source], fr2.at[source], f2_s.at[by], f2_r.at[source],
                   y_peer(by)).wait_recv()
            f2_copy(by).wait_send()
        fr3[z] = slots_sum(fr2, 4).astype(BF16)
        for by in range(1, 4):
            f3_copy(by).start()

    def start_f4():
        for by in range(1, 4):
            source = lax.rem(z + by, 4)
            remote(fr3.at[source], fr3.at[source], f3_s.at[by], f3_r.at[source],
                   z_peer(by)).wait_recv()
            f3_copy(by).wait_send()
        fr4[me] = (slots_sum(fr3, 4) * norm).astype(BF16)
        for by in range(1, 8):
            f4_copy(by).start()

    def end_f4():
        for by in range(1, 8):
            source = member_peer(by)
            remote(fr4.at[source], fr4.at[source], f4_s.at[by], f4_r.at[source],
                   (source, mp)).wait_recv()
            f4_copy(by).wait_send()
        for j in range(MEMBERS):
            gf_ref[:, 128 * j:128 * j + 128] = fr4[j, pl.ds(0, 100), :].astype(F32)

    make_dmix(0)
    attend_back(1, (0,))
    make_dmix(1)

    for at in range(2):
        value = dot(dmix[pl.ds(512 * at, 512), :], att[...], NT)
        for k in range(2):
            store_unit(w_g, 2 * at + k, value[256 * k:256 * k + 256])
    core_copy(0).start()
    g_fields = dot(dpf[pl.ds(0, FIELD_ROWS), :], mix[...], NT)
    for j in range(MEMBERS):
        fs[j] = g_fields[:, 128 * j:128 * j + 128].astype(BF16)
    for by in range(1, 8):
        f1_copy(by).start()
    fr1[me] = fs[me]

    attend_back(1, (1,))
    scatter(1)
    start_one(0)
    attend_back(2, (0, 1))
    scatter(2)
    query_grad(1)
    attend_back(3, (0, 1))
    start_f2()
    start_one(1)
    scatter(3)
    query_grad(2)
    start_two(0)
    attend_back(4, (0, 1))
    start_f3()
    start_one(2)
    scatter(4)
    query_grad(3)
    query_grad(4)
    start_two(1)
    start_x(0)

    def back_copy(r):
        return remote(
            outgo.at[pl.ds(32 * r, 32)], drecv.at[pl.ds(32 * (3 - r), 32)],
            back_s.at[r], back_r.at[3 - r], halo_peer(OFFSETS[r]),
        )

    through_kv = dot(dkfull[...], wkv_v[...])
    outgo[...] = through_kv[128:].astype(BF16)
    own_hidden = through_kv[:128]
    for r in range(4):
        back_copy(r).start()
    start_one(3)
    start_direct()

    stage = att

    def out_copy(at):
        return pltpu.make_async_copy(
            stage.at[part(at, 256)], dgrid_hbm.at[part(at, 256)], out_sem.at[at]
        )

    def grid_grad(at):
        span = pl.ds(256 * at, 256)
        through = dot(dq[:, span].T, wq_v[...])
        direct = dot(dpf[:, span].T, wfp[...]).astype(BF16).astype(F32)
        stage[span, :] = (direct + through).astype(BF16)
        out_copy(at).start()

    grid_grad(0)
    start_two(2)
    start_f4()
    start_x(1)

    loads[5].wait()
    for by in range(4):
        source = 2 * lax.rem(x + by, 4) + other
        share(source, 0, sibling).wait_recv()
    wait_keyval()
    for m in range(MEMBERS):
        rows = pl.ds(128 * m, 128)
        kvr[rows, :] = (
            kvr[rows, :].astype(F32) + dot(halo_home, kvh[rows, :])
        ).astype(BF16)
    value = dot(kvr[...].T, hall[...])
    k_own[0, 0] = value[:, :512].astype(BF16)
    k_own[1, 0] = (
        value[:, 512:].reshape(4, 4, 16, 512).transpose(1, 0, 2, 3).reshape(256, 512)
    ).astype(BF16)
    for half in range(2):
        for by in (2, 1, 3):
            one_copy(5, half, by).start()

    grid_grad(1)
    start_x(2)
    start_two(3)
    grid_grad(2)
    for r in range(4):
        back_copy(r).wait()
    dhid_ref[...] = (own_hidden + dot(halo_home, drecv[...])).astype(BF16)
    start_two(5)
    grid_grad(3)
    end_direct()
    start_x(3)
    end_f4()
    end_keyval()
    for half in range(2):
        for by in (1, 3, 2):
            two_copy(5, half, by).wait()
        gkv_ref[:, 512 * half:512 * half + 512] = finish_two(5, half, 0) * norm
    for n in range(5):
        end_x(n)
    for by in range(1, 4):
        share(x_peer(by), 3 + by, sibling).wait_send()
    for kind in range(2):
        for by in range(1, 8):
            source = member_peer(by)
            remote(rx.at[kind, source], rx.at[kind, source], x_s.at[0, 0],
                   x_r.at[kind, source], (source, mp)).wait_recv()
    for kind, ref in ((0, go_ref), (1, gq_ref)):
        for half in range(2):
            total = rx[kind, half].astype(F32)
            for by in range(1, 4):
                total = total + rx[kind, 2 * by + half].astype(F32)
            total = total * norm
            ref[:, 512 * half:512 * half + 512] = jnp.where(c == 0, total[:8], total[8:])
    for at in range(4):
        out_copy(at).wait()


def hand_over(*refs):
    count = 6
    sources, targets, held = refs[:count], refs[count:2 * count], refs[2 * count:3 * count]
    in_sems, out_sems = refs[3 * count:]
    pieces = [(1, part(at, 256)) for at in range(4)] + [
        (n, slice(None)) for n in (5, 0, 3, 2, 4)
    ]
    reads = [
        pltpu.make_async_copy(sources[n].at[rows], held[n].at[rows], in_sems.at[i])
        for i, (n, rows) in enumerate(pieces)
    ]
    writes = [
        pltpu.make_async_copy(held[n].at[rows], targets[n].at[rows], out_sems.at[i])
        for i, (n, rows) in enumerate(pieces)
    ]
    for read in reads:
        read.start()
    for read, write in zip(reads, writes):
        read.wait()
        write.start()
    for write in writes:
        write.wait()


def on_device(
    hidden, grid_emb, targets, area_w, field_w, edge_table, halo_rows,
    w_query, w_keyval, w_attn_out, w_fields,
):
    def vm(*shape, dtype=BF16):
        return pltpu.VMEM(shape, dtype)

    def sems(*shape):
        return pltpu.SemaphoreType.DMA(shape)

    def comm(lead, count):
        return [
            vm(*lead, 2, 2, count, 256, 256), vm(*lead, 2, count, 256, 256),
            vm(*lead, 2, 3, count, 64, 256), vm(*lead, 2, count, 64, 256),
            vm(*lead, 2, 3, count, 16, 256), vm(*lead, count, 16, 512),
        ]

    square = (1024, 1024)
    scratch = [
        vm(*square), vm(*square), vm(2048, 1024), vm(*square), vm(*square),
        vm(*square), vm(*square), vm(*square), vm(*square),
        vm(256, 1024), vm(2048, 256), vm(3, 256, 1024), vm(3, 2048, 1024),
        vm(16, 8, 1024, dtype=F32),
        vm(128, 1024), vm(1024, 128), vm(8, 128, dtype=F32), vm(128, 128, dtype=F32),
        vm(128, 1024, dtype=F32), vm(2, 128, TILE, dtype=F32), vm(2, 8, 16, TILE, dtype=F32),
        vm(2, 8, 16, TILE), vm(128, 1024),
        vm(256, 1024, dtype=F32), vm(512, 1024), vm(128, 1024), vm(*square), vm(*square),
        vm(128, 1024), vm(256, 2048), vm(1024, 256), vm(1024, 256), vm(15, 2, 16, 256),
        vm(8, FIELD_ROWS, 128), vm(8, FIELD_ROWS, 128), vm(4, FIELD_ROWS, 128),
        vm(4, FIELD_ROWS, 128), vm(8, FIELD_ROWS, 128),
        *comm((), 4), *comm((4,), 1),
        vm(2, 1, 256, 512), vm(2, 3, 1, 64, 512), vm(2, 1, 64, 512), vm(2, 3, 1, 16, 512),
        vm(2, 8, 16, 512),
        sems(6), sems(4), sems(4), sems(7), sems(8), sems(2, 8), sems(2, 8), sems(2, 8),
        sems(2, 8), sems(4), sems(4), sems(4, 2), sems(8), sems(4, 2, 4), sems(8, 4),
        sems(15), sems(15),
        sems(8), sems(8), sems(4), sems(4), sems(4), sems(4), sems(8), sems(8),
        sems(5), sems(5), sems(6, 2, 3), sems(6, 2, 3), sems(6, 2, 3), sems(6, 2, 3),
        sems(5, 8), sems(2, 8), sems(4),
    ]
    vmem = pl.BlockSpec(memory_space=pltpu.VMEM)
    hbm = pl.BlockSpec(memory_space=pl.ANY)
    shapes = (
        jax.ShapeDtypeStruct((128, 1024), BF16),
        jax.ShapeDtypeStruct(square, BF16),
        jax.ShapeDtypeStruct((8, 1024), F32),
        jax.ShapeDtypeStruct((16, 1024), F32),
        jax.ShapeDtypeStruct((8, 1024), F32),
        jax.ShapeDtypeStruct((100, 1024), F32),
    )
    raw = pl.pallas_call(
        kernel,
        out_shape=shapes,
        in_specs=[hbm, hbm, vmem, vmem, vmem, vmem, vmem, hbm, hbm, hbm, vmem],
        out_specs=(vmem, hbm, vmem, vmem, vmem, vmem),
        scratch_shapes=scratch,
        compiler_params=pltpu.CompilerParams(
            collective_id=0, has_side_effects=True, vmem_limit_bytes=63 * 1024 * 1024
        ),
        cost_estimate=pl.CostEstimate(
            flops=22_000_000_000, bytes_accessed=16_000_000, transcendentals=500_000
        ),
        name="decoder_backward",
    )(
        hidden[0], grid_emb[0], targets, area_w.reshape(1, 1024), field_w.reshape(1, 100),
        edge_table.T, halo_rows, w_query, w_keyval, w_attn_out, w_fields,
    )
    outs = pl.pallas_call(
        hand_over,
        out_shape=shapes,
        in_specs=[hbm] * 6,
        out_specs=(hbm,) * 6,
        scratch_shapes=[pltpu.VMEM(shape.shape, shape.dtype) for shape in shapes]
        + [sems(9), sems(9)],
        compiler_params=pltpu.CompilerParams(vmem_limit_bytes=63 * 1024 * 1024),
        cost_estimate=pl.CostEstimate(flops=0, bytes_accessed=6_000_000, transcendentals=0),
        name="hand_over",
    )(*raw)
    return (outs[0][None], outs[1][None], *outs[2:])


def solution(mesh):
    in_specs = (
        P("member", "mp", None),
        P("member", "mp", None),
        P(None, "mp"),
        P("mp"),
        P(),
        P("mp", None),
        P("mp", None),
        P(),
        P(),
        P(),
        P(),
    )
    out_specs = (
        P("member", "mp", None),
        P("member", "mp", None),
        P(("member", "mp"), None),
        P(("member", "mp"), None),
        P(("member", "mp"), None),
        P(),
    )
    return jax.shard_map(
        on_device, mesh=mesh, in_specs=in_specs, out_specs=out_specs, check_vma=False
    )
```

time: 116 us -> 96.7 us (0.83)
  local copies, waits for them, and re-layouts: 12 us -> 0 us
  Pallas kernels: 103 us -> 95.4 us
    unnamed x15 -> x0, local copies, waits for them, and re-layouts: 9.17 us -> none
    pallas_call x1 -> x2, Pallas kernels: 103 us -> 95.4 us  [the longest x1 92.7 us: on_device(): pl.pallas_call(kernel, out_shape=shapes, in_specs=[hbm, hbm, vmem, vmem,...]
    reshape x3 -> x0, local copies, waits for them, and re-layouts: 2.81 us -> none  [the longest x1 1.42 us: on_device(): halo_rows.reshape(128, 1)]
where the time goes in v2:
time: 96.7 us; the launch traced here: 96.3 us
  Pallas kernels  95.4 us (99%)
    pallas_call x1, Pallas kernels, on_device(): pl.pallas_call(kernel, out_shape=shapes, in_specs=[hbm, hbm, vmem, vmem,...  92.7 us
    pallas_call x1, Pallas kernels, on_device(): pl.pallas_call(hand_over, out_shape=shapes, in_specs=[hbm] * 6, out_specs...  2.76 us

profile of v2, /device:TPU:1, one launch (start us, length us, event | category | flops | bytes accessed | tf_op | source)
XLA Modules:
  0.0 96.3 jit_solution(14026229267624347286)
XLA Ops:
  0.6 92.7 %decoder_backward.1 = (bf16[128,1024]{1,0:T(8,128)(2,1)}, bf16[1024,1024]{1,0:T(8,128)(2,1)}, f32[8,1024]{1,0:T(8,128)}, f32[16,1024]{1,0:T(8,128)}, f32[8,1024]{1,0:T(8,128)}, /*index=5*/f32[100,1024]{1,0:T(8,128)}) custom-call(bf16[128,1024]{1,0:T(8,128)(2,1)} %bitcast.9, bf16[1024,1024]{1,0:T(8,128)(2,1)} %bitcast.7, f32[100,1024]{1,0:T(8,128)} %tgt_ref.1, ...), custom_call_target="tpu_custom_call" | custom-call | flops 22000001024 | bytes 16000000 | tf_op jit(solution)/shard_map/decoder_backward/pallas_call | solution.py:775
  93.3 2.8 %hand_over.1 = (bf16[128,1024]{1,0:T(8,128)(2,1)}, bf16[1024,1024]{1,0:T(8,128)(2,1)}, f32[8,1024]{1,0:T(8,128)}, f32[16,1024]{1,0:T(8,128)}, f32[8,1024]{1,0:T(8,128)}, /*index=5*/f32[100,1024]{1,0:T(8,128)}) custom-call(bf16[128,1024]{1,0:T(8,128)(2,1)} %get-tuple-element.18.refs_0_, bf16[1024,1024]{1,0:T(8,128)(2,1)} %get-tuple-element.19.refs_1_, ...), custom_call_target="tpu_custom_call" | custom-call | bytes 6000000 | tf_op jit(solution)/shard_map/hand_over/pallas_call | solution.py:792

commit v3 on v2

--- a/solution.py
+++ b/solution.py
@@ -41,12 +41,13 @@
 
 
 def kernel(
-    hid_hbm, grid_hbm, tgt_ref, area_ref, field_ref, edge_ref, halo_ref,
-    wq_hbm, wkv_hbm, wo_hbm, wf_ref,
-    dhid_ref, dgrid_hbm, gq_ref, gkv_ref, go_ref, gf_ref,
+    hid_hbm, grid_hbm, tgt_hbm, area_ref, field_ref, edge_ref, halo_ref,
+    wq_hbm, wkv_hbm, wo_hbm, wf_hbm,
+    dhid_hbm, dgrid_hbm, gq_ref, gkv_ref, go_ref, gf_hbm,
+    tgt_ref, wf_ref, dhid_ref, gf_ref,
     grid_v, wq_v, wkv_v, wo_v, wot_v, tgrid, qt, att, mix, th, tkv, oh, kvg, wts,
     wfp, wft, frow, fcol, tpad, preds, predr, dps, dpf,
-    datt, dkv_last, outgo, hall, dq,
+    datt, dpart, outgo, hall, dq,
     drecv, dkfull, kvr, kvh, direct,
     fs, fr1, fr2, fr3, fr4,
     w_g, w_recv, w_r1, w_s1, w_r2, w_fin,
@@ -92,15 +93,16 @@
         for n, (src, dst) in enumerate((
             (hid_hbm, th.at[pl.ds(0, 128)]), (grid_hbm, grid_v), (wq_hbm, wq_v),
             (wkv_hbm, wkv_v), (wo_hbm, wo_v), (hid_hbm, hall.at[part(me, 128)]),
+            (tgt_hbm, tgt_ref), (wf_hbm, wf_ref),
         ))
     ]
     for load in loads:
         load.start()
     barrier = pltpu.get_barrier_semaphore()
     partners = (
-        [(me, lax.rem(mp + by, 16)) for by in range(1, 16)]
+        [halo_peer(by) for by in OFFSETS]
         + [(member_peer(by), mp) for by in range(1, 8)]
-        + [(member_peer(by), halo_peer(far)[1]) for by in range(1, 8) for far in OFFSETS]
+        + [y_peer(by) for by in range(1, 4)]
     )
     for partner in partners:
         pl.semaphore_signal(barrier, inc=1, device_id=partner, device_id_type=MESH)
@@ -109,11 +111,10 @@
         oh[e] = (
             lax.broadcasted_iota(jnp.int32, (256, 1024), 0) == edge_ref[e:e + 1, :]
         ).astype(BF16)
+    loads[7].wait()
     wfp[...] = jnp.zeros_like(wfp)
     wfp[pl.ds(0, 100), :] = wf_ref[...]
     wft[...] = wfp[...].T
-    tpad[...] = jnp.zeros_like(tpad)
-    tpad[pl.ds(0, 100), :] = tgt_ref[...]
     frow[...] = jnp.zeros_like(frow)
     frow[pl.ds(0, 1), pl.ds(0, 100)] = field_ref[...]
     fcol[...] = jnp.broadcast_to(frow[pl.ds(0, 1), :], (128, 128)).T
@@ -154,13 +155,26 @@
         lanes = pl.ds(TILE * at, TILE)
         qt[:, lanes] = dot(wq_v[...], tgrid[:, lanes]).astype(BF16)
 
+    def make_table(first):
+        rows = pl.ds(first, 128)
+
+        def rows_of(at):
+            tkv[part(at, 512), rows] = dot(wkv_v[part(at, 512), :], th[rows, :], NT).astype(BF16)
+        blocks(4, rows_of)
+
     loads[3].wait()
+    make_table(0)
+    loads[4].wait()
+
+    def turn_out(at):
+        wot_v[:, part(at, 256)] = wo_v[part(at, 256), :].T
+    blocks(4, turn_out)
     for copy in halos:
         copy.wait()
-
-    def make_table(at):
-        tkv[part(at, 512), :] = dot(wkv_v[part(at, 512), :], th[...], NT).astype(BF16)
-    blocks(4, make_table)
+    make_table(128)
+    loads[6].wait()
+    tpad[...] = jnp.zeros_like(tpad)
+    tpad[pl.ds(0, 100), :] = tgt_ref[...]
 
     def gather(t):
         lanes = pl.ds(t * TILE, TILE)
@@ -258,63 +272,61 @@
         blocks(2, rows_of)
 
     gather(0)
-    loads[4].wait()
     attend(0)
     predict(0)
     gather(1)
+    attend(1)
     crps(0)
-    attend(1)
     predict(1)
 
-    def turn_out(at):
-        wot_v[:, part(at, 256)] = wo_v[part(at, 256), :].T
-    blocks(4, turn_out)
     for by in range(1, 4):
         source = x_peer(by)
         share(me, by, (x_peer(by), mp)).wait_send()
         share(source, 0, sibling).wait_recv()
         share(source, 3 + by, sibling).start()
     share(me, 0, sibling).wait_send()
-    crps(1)
-
-    dkv = (wo_v.at[pl.ds(0, 512)], wo_v.at[pl.ds(512, 512)], dkv_last)
+
+    dkv = [
+        wo_v.at[pl.ds(512 * (e // 2), 512), pl.ds(512 * (e % 2), 512)] for e in range(3)
+    ]
 
     def block_of(n):
         return lax.rem(x + n, 4)
 
-    def attend_back(n, tiles):
+    def attend_back(n, t):
         j = block_of(n)
         base = pl.multiple_of(j * 256, 256)
-        span = pl.ds(tiles[0] * TILE, len(tiles) * TILE)
-        datt[:, span] = dot(wot_v[pl.ds(base, 256), :], dmix[:, span])
-        for t in tiles:
-            lanes = pl.ds(t * TILE, TILE)
-
-            def head(hh):
-                local, vlocal = part(hh, 64), part(hh, 64, 256)
-                rows = pl.ds(pl.multiple_of(base + hh * 64, 64), 64)
-                vrows = pl.ds(pl.multiple_of(1024 + base + hh * 64, 64), 64)
-                grad = datt[local, lanes]
-                query = qt[rows, lanes].astype(F32)
-                weight = [wts[4 * j + hh, e:e + 1, lanes] for e in range(3)]
-                d_weight = [
-                    jnp.sum(grad * kvg[e, vrows, lanes].astype(F32), axis=0, keepdims=True)
-                    for e in range(3)
-                ]
-                inner = (
-                    weight[0] * d_weight[0] + weight[1] * d_weight[1] + weight[2] * d_weight[2]
-                )
-                out = None
-                for e in range(3):
-                    d_score = weight[e] * (d_weight[e] - inner) * 0.125
-                    term = d_score * kvg[e, rows, lanes].astype(F32)
-                    out = term if out is None else out + term
-                    dkv[e][local, lanes] = (d_score * query).astype(BF16)
-                    dkv[e][vlocal, lanes] = (
-                        weight[e].astype(BF16).astype(F32) * grad
-                    ).astype(BF16)
-                dq[rows, lanes] = out.astype(BF16)
-            blocks(4, head)
+        lanes = pl.ds(t * TILE, TILE)
+        datt[...] = dot(wot_v[pl.ds(base, 256), :], dmix[:, lanes])
+
+        def head(hh):
+            local, vlocal = part(hh, 64), part(hh, 64, 256)
+            rows = pl.ds(pl.multiple_of(base + hh * 64, 64), 64)
+            vrows = pl.ds(pl.multiple_of(1024 + base + hh * 64, 64), 64)
+            grad = datt[local, :]
+            query = qt[rows, lanes].astype(F32)
+            weight = [wts[4 * j + hh, e:e + 1, lanes] for e in range(3)]
+            d_weight = [
+                jnp.sum(grad * kvg[e, vrows, lanes].astype(F32), axis=0, keepdims=True)
+                for e in range(3)
+            ]
+            inner = weight[0] * d_weight[0] + weight[1] * d_weight[1] + weight[2] * d_weight[2]
+            out = None
+            for e in range(3):
+                d_score = weight[e] * (d_weight[e] - inner) * 0.125
+                term = d_score * kvg[e, rows, lanes].astype(F32)
+                out = term if out is None else out + term
+                dkv[e][local, :] = (d_score * query).astype(BF16)
+                dkv[e][vlocal, :] = (weight[e].astype(BF16).astype(F32) * grad).astype(BF16)
+            dq[rows, lanes] = out.astype(BF16)
+        blocks(4, head)
+        total = dot(oh[0, :, lanes], dkv[0][...], NT)
+        for e in range(1, 3):
+            total = total + dot(oh[e, :, lanes], dkv[e][...], NT)
+        if t == 0:
+            dpart[n - 1] = total
+        else:
+            send_keyval(n, total + dpart[n - 1])
 
     def kv_targets(n):
         j = block_of(n)
@@ -336,10 +348,7 @@
             (target, halo_peer(OFFSETS[r])[1]),
         )
 
-    def scatter(n):
-        total = dot(oh[0], dkv[0][...], NT)
-        for e in range(1, 3):
-            total = total + dot(oh[e], dkv[e][...], NT)
+    def send_keyval(n, total):
         for which in range(2):
             target = kv_targets(n)[which]
             piece = total[:, 256 * which:256 * which + 256].astype(BF16)
@@ -386,7 +395,8 @@
                 at = 512 * core + 256 * half
                 piece = value[:, at:at + 256].reshape(2, 4, 4, 8, 256)
                 order = (2, 1, 0, 3, 4) if half == 1 and crossed else (1, 2, 0, 3, 4)
-                ref[core, half, unit] = piece.transpose(order).reshape(256, 256).astype(BF16)
+                piece = piece.transpose(order).reshape(256, 256)
+                ref[core, half, unit] = piece.astype(BF16)
 
     units = [4, 1, 1, 1, 1, 1]
     sets = [(w_g, w_recv, w_g.at[c], w_r1, w_s1, w_r2, w_fin)] + [
@@ -514,6 +524,21 @@
         store_unit(sets[n][0], 0, dot(dq[span, :], grid_v[...]), n < 4)
         core_copy(n).start()
 
+    def out_grad():
+        for at in range(2):
+            value = dot(dmix[pl.ds(512 * at, 512), :], att[...], NT)
+            for k in range(2):
+                store_unit(w_g, 2 * at + k, value[256 * k:256 * k + 256])
+        core_copy(0).start()
+
+    def fields_grad():
+        value = dot(dpf[pl.ds(0, FIELD_ROWS), :], mix[...], NT)
+        for j in range(MEMBERS):
+            fs[j] = value[:, 128 * j:128 * j + 128].astype(BF16)
+        for by in range(1, 8):
+            f1_copy(by).start()
+        fr1[me] = fs[me]
+
     def f1_copy(by):
         target = member_peer(by)
         return remote(fs.at[target], fr1.at[me], f1_s.at[by], f1_r.at[me], (target, mp))
@@ -573,41 +598,27 @@
             gf_ref[:, 128 * j:128 * j + 128] = fr4[j, pl.ds(0, 100), :].astype(F32)
 
     make_dmix(0)
-    attend_back(1, (0,))
+    attend_back(1, 0)
+    crps(1)
+    attend_back(2, 0)
+    attend_back(3, 0)
+    attend_back(4, 0)
     make_dmix(1)
-
-    for at in range(2):
-        value = dot(dmix[pl.ds(512 * at, 512), :], att[...], NT)
-        for k in range(2):
-            store_unit(w_g, 2 * at + k, value[256 * k:256 * k + 256])
-    core_copy(0).start()
-    g_fields = dot(dpf[pl.ds(0, FIELD_ROWS), :], mix[...], NT)
-    for j in range(MEMBERS):
-        fs[j] = g_fields[:, 128 * j:128 * j + 128].astype(BF16)
-    for by in range(1, 8):
-        f1_copy(by).start()
-    fr1[me] = fs[me]
-
-    attend_back(1, (1,))
-    scatter(1)
+    out_grad()
+    fields_grad()
+    attend_back(1, 1)
     start_one(0)
-    attend_back(2, (0, 1))
-    scatter(2)
     query_grad(1)
-    attend_back(3, (0, 1))
+    attend_back(2, 1)
+    query_grad(2)
+    start_one(1)
+    attend_back(3, 1)
+    query_grad(3)
     start_f2()
-    start_one(1)
-    scatter(3)
-    query_grad(2)
-    start_two(0)
-    attend_back(4, (0, 1))
-    start_f3()
     start_one(2)
-    scatter(4)
-    query_grad(3)
+    attend_back(4, 1)
     query_grad(4)
-    start_two(1)
-    start_x(0)
+    start_one(3)
 
     def back_copy(r):
         return remote(
@@ -620,7 +631,6 @@
     own_hidden = through_kv[:128]
     for r in range(4):
         back_copy(r).start()
-    start_one(3)
     start_direct()
 
     stage = att
@@ -638,9 +648,10 @@
         out_copy(at).start()
 
     grid_grad(0)
-    start_two(2)
-    start_f4()
-    start_x(1)
+    start_two(0)
+    start_two(1)
+    grid_grad(1)
+    start_f3()
 
     loads[5].wait()
     for by in range(4):
@@ -661,18 +672,25 @@
         for by in (2, 1, 3):
             one_copy(5, half, by).start()
 
-    grid_grad(1)
-    start_x(2)
+    start_two(2)
     start_two(3)
     grid_grad(2)
+    start_x(0)
+    start_x(1)
     for r in range(4):
         back_copy(r).wait()
     dhid_ref[...] = (own_hidden + dot(halo_home, drecv[...])).astype(BF16)
+    dhid_out = pltpu.make_async_copy(dhid_ref, dhid_hbm, out_sem.at[4])
+    dhid_out.start()
+    start_f4()
+    grid_grad(3)
     start_two(5)
-    grid_grad(3)
+    start_x(2)
+    start_x(3)
     end_direct()
-    start_x(3)
     end_f4()
+    gf_out = pltpu.make_async_copy(gf_ref, gf_hbm, out_sem.at[5])
+    gf_out.start()
     end_keyval()
     for half in range(2):
         for by in (1, 3, 2):
@@ -696,6 +714,8 @@
             ref[:, 512 * half:512 * half + 512] = jnp.where(c == 0, total[:8], total[8:])
     for at in range(4):
         out_copy(at).wait()
+    dhid_out.wait()
+    gf_out.wait()
 
 
 def hand_over(*refs):
@@ -741,6 +761,7 @@
 
     square = (1024, 1024)
     scratch = [
+        vm(100, 1024, dtype=F32), vm(100, 1024), vm(128, 1024), vm(100, 1024, dtype=F32),
         vm(*square), vm(*square), vm(2048, 1024), vm(*square), vm(*square),
         vm(*square), vm(*square), vm(*square), vm(*square),
         vm(256, 1024), vm(2048, 256), vm(3, 256, 1024), vm(3, 2048, 1024),
@@ -748,19 +769,19 @@
         vm(128, 1024), vm(1024, 128), vm(8, 128, dtype=F32), vm(128, 128, dtype=F32),
         vm(128, 1024, dtype=F32), vm(2, 128, TILE, dtype=F32), vm(2, 8, 16, TILE, dtype=F32),
         vm(2, 8, 16, TILE), vm(128, 1024),
-        vm(256, 1024, dtype=F32), vm(512, 1024), vm(128, 1024), vm(*square), vm(*square),
+        vm(256, TILE, dtype=F32), vm(4, 256, 512, dtype=F32), vm(128, 1024), vm(*square), vm(*square),
         vm(128, 1024), vm(256, 2048), vm(1024, 256), vm(1024, 256), vm(15, 2, 16, 256),
         vm(8, FIELD_ROWS, 128), vm(8, FIELD_ROWS, 128), vm(4, FIELD_ROWS, 128),
         vm(4, FIELD_ROWS, 128), vm(8, FIELD_ROWS, 128),
         *comm((), 4), *comm((4,), 1),
         vm(2, 1, 256, 512), vm(2, 3, 1, 64, 512), vm(2, 1, 64, 512), vm(2, 3, 1, 16, 512),
         vm(2, 8, 16, 512),
-        sems(6), sems(4), sems(4), sems(7), sems(8), sems(2, 8), sems(2, 8), sems(2, 8),
+        sems(8), sems(4), sems(4), sems(7), sems(8), sems(2, 8), sems(2, 8), sems(2, 8),
         sems(2, 8), sems(4), sems(4), sems(4, 2), sems(8), sems(4, 2, 4), sems(8, 4),
         sems(15), sems(15),
         sems(8), sems(8), sems(4), sems(4), sems(4), sems(4), sems(8), sems(8),
         sems(5), sems(5), sems(6, 2, 3), sems(6, 2, 3), sems(6, 2, 3), sems(6, 2, 3),
-        sems(5, 8), sems(2, 8), sems(4),
+        sems(5, 8), sems(2, 8), sems(6),
     ]
     vmem = pl.BlockSpec(memory_space=pltpu.VMEM)
     hbm = pl.BlockSpec(memory_space=pl.ANY)
@@ -775,8 +796,8 @@
     raw = pl.pallas_call(
         kernel,
         out_shape=shapes,
-        in_specs=[hbm, hbm, vmem, vmem, vmem, vmem, vmem, hbm, hbm, hbm, vmem],
-        out_specs=(vmem, hbm, vmem, vmem, vmem, vmem),
+        in_specs=[hbm, hbm, hbm, vmem, vmem, vmem, vmem, hbm, hbm, hbm, hbm],
+        out_specs=(hbm, hbm, vmem, vmem, vmem, hbm),
         scratch_shapes=scratch,
         compiler_params=pltpu.CompilerParams(
             collective_id=0, has_side_effects=True, vmem_limit_bytes=63 * 1024 * 1024

time: 96.7 us -> 95.2 us (0.984)
  Pallas kernels: 95.4 us -> 94.2 us
    pallas_call x1, Pallas kernels: 92.7 us -> 91.4 us  [on_device(): pl.pallas_call(kernel, out_shape=shapes, in_specs=[hbm, hbm, hbm, vmem, v...]
where the time goes in v3:
time: 95.2 us; the launch traced here: 95 us
  Pallas kernels  94.2 us (99%)
    pallas_call x1, Pallas kernels, on_device(): pl.pallas_call(kernel, out_shape=shapes, in_specs=[hbm, hbm, hbm, vmem, v...  91.4 us
    pallas_call x1, Pallas kernels, on_device(): pl.pallas_call(hand_over, out_shape=shapes, in_specs=[hbm] * 6, out_specs...  2.76 us

profile of v3, /device:TPU:1, one launch (start us, length us, event | category | flops | bytes accessed | tf_op | source)
XLA Modules:
  0.0 95.0 jit_solution(2830698868079468570)
XLA Ops:
  0.6 91.4 %decoder_backward.1 = (bf16[128,1024]{1,0:T(8,128)(2,1)}, bf16[1024,1024]{1,0:T(8,128)(2,1)}, f32[8,1024]{1,0:T(8,128)}, f32[16,1024]{1,0:T(8,128)}, f32[8,1024]{1,0:T(8,128)}, /*index=5*/f32[100,1024]{1,0:T(8,128)}) custom-call(bf16[128,1024]{1,0:T(8,128)(2,1)} %bitcast.9, bf16[1024,1024]{1,0:T(8,128)(2,1)} %bitcast.7, f32[100,1024]{1,0:T(8,128)} %tgt_hbm.1, ...), custom_call_target="tpu_custom_call" | custom-call | flops 22000001024 | bytes 16000000 | tf_op jit(solution)/shard_map/decoder_backward/pallas_call | solution.py:796
  92.0 2.8 %hand_over.1 = (bf16[128,1024]{1,0:T(8,128)(2,1)}, bf16[1024,1024]{1,0:T(8,128)(2,1)}, f32[8,1024]{1,0:T(8,128)}, f32[16,1024]{1,0:T(8,128)}, f32[8,1024]{1,0:T(8,128)}, /*index=5*/f32[100,1024]{1,0:T(8,128)}) custom-call(bf16[128,1024]{1,0:T(8,128)(2,1)} %get-tuple-element.18.refs_0_, bf16[1024,1024]{1,0:T(8,128)(2,1)} %get-tuple-element.19.refs_1_, ...), custom_call_target="tpu_custom_call" | custom-call | bytes 6000000 | tf_op jit(solution)/shard_map/hand_over/pallas_call | solution.py:813

commit v4 on v3

--- a/solution.py
+++ b/solution.py
@@ -652,6 +652,11 @@
     start_two(1)
     grid_grad(1)
     start_f3()
+    start_two(2)
+    start_two(3)
+    grid_grad(2)
+    start_x(0)
+    start_x(1)
 
     loads[5].wait()
     for by in range(4):
@@ -672,11 +677,6 @@
         for by in (2, 1, 3):
             one_copy(5, half, by).start()
 
-    start_two(2)
-    start_two(3)
-    grid_grad(2)
-    start_x(0)
-    start_x(1)
     for r in range(4):
         back_copy(r).wait()
     dhid_ref[...] = (own_hidden + dot(halo_home, drecv[...])).astype(BF16)

time: 95.2 us -> 97.8 us (1.027)
  Pallas kernels: 94.2 us -> 96.8 us
    pallas_call x1, Pallas kernels: 91.4 us -> 94 us  [on_device(): pl.pallas_call(kernel, out_shape=shapes, in_specs=[hbm, hbm, hbm, vmem, v...]
where the time goes in v4:
time: 97.8 us; the launch traced here: 97.6 us
  Pallas kernels  96.8 us (99%)
    pallas_call x1, Pallas kernels, on_device(): pl.pallas_call(kernel, out_shape=shapes, in_specs=[hbm, hbm, hbm, vmem, v...  94 us
    pallas_call x1, Pallas kernels, on_device(): pl.pallas_call(hand_over, out_shape=shapes, in_specs=[hbm] * 6, out_specs...  2.76 us

profile of v4, /device:TPU:1, one launch (start us, length us, event | category | flops | bytes accessed | tf_op | source)
XLA Modules:
  0.0 97.6 jit_solution(6322008225425203589)
XLA Ops:
  0.6 94.0 %decoder_backward.1 = (bf16[128,1024]{1,0:T(8,128)(2,1)}, bf16[1024,1024]{1,0:T(8,128)(2,1)}, f32[8,1024]{1,0:T(8,128)}, f32[16,1024]{1,0:T(8,128)}, f32[8,1024]{1,0:T(8,128)}, /*index=5*/f32[100,1024]{1,0:T(8,128)}) custom-call(bf16[128,1024]{1,0:T(8,128)(2,1)} %bitcast.9, bf16[1024,1024]{1,0:T(8,128)(2,1)} %bitcast.7, f32[100,1024]{1,0:T(8,128)} %tgt_hbm.1, ...), custom_call_target="tpu_custom_call" | custom-call | flops 22000001024 | bytes 16000000 | tf_op jit(solution)/shard_map/decoder_backward/pallas_call | solution.py:796
  94.7 2.8 %hand_over.1 = (bf16[128,1024]{1,0:T(8,128)(2,1)}, bf16[1024,1024]{1,0:T(8,128)(2,1)}, f32[8,1024]{1,0:T(8,128)}, f32[16,1024]{1,0:T(8,128)}, f32[8,1024]{1,0:T(8,128)}, /*index=5*/f32[100,1024]{1,0:T(8,128)}) custom-call(bf16[128,1024]{1,0:T(8,128)(2,1)} %get-tuple-element.18.refs_0_, bf16[1024,1024]{1,0:T(8,128)(2,1)} %get-tuple-element.19.refs_1_, ...), custom_call_target="tpu_custom_call" | custom-call | bytes 6000000 | tf_op jit(solution)/shard_map/hand_over/pallas_call | solution.py:813
